TPU v7x, 256 devices: a whole 4x4x8 slice. The times are simulated.
256 devices in a mesh: dp: 8 (over z), expert: 32 (over y, x, core).
Axes of the slice: x: 4, y: 4, z: 8, core: 2. Of those that a mesh axis runs over, the one named last changes fastest.
Arguments:
- tokens: bfloat16 [16384, 2048], P(('dp', 'expert')), may hold values from -6 to 6
- row_cotangent: bfloat16 [16384, 8, 768], P(('dp', 'expert')), may hold values from -6 to 6
- routes: int32 [16384, 8], P(('dp', 'expert')), may hold values from 0 to 63, all different within a row; in each aligned block of 64 rows (0 to 63, 64 to 127, ...) at most 12 rows name the same one
- w_gate: bfloat16 [32, 2048, 768], P('expert'), may hold values from -0.125 to 0.125
- w_up: bfloat16 [32, 2048, 768], P('expert'), may hold values from -0.125 to 0.125
Outputs:
- grad_tokens: bfloat16 [16384, 2048], P(('dp', 'expert'))
- grad_gate: float32 [32, 2048, 768], P('expert', 'dp')
- grad_up: float32 [32, 2048, 768], P('expert', 'dp')
Inputs may be any that keep to these rules, and one draw needn't show every extreme that they name: A token's 8 routes name distinct copies. Within the 64 tokens of one device no route is named by more than 12 tokens, a bound that some block reaches.
All inputs are finite; a program needn't handle non-finite values.
Results may differ from a plain program's by a relative error of at most 0.018.
Values may be sent and summed in bfloat16 or wider, within the bound.
A program may use at most 128 MiB of HBM per device.

v0:
```python
import jax
import jax.numpy as jnp
from jax import lax
from jax.sharding import PartitionSpec as P


def partner(x, axis, distance):
    return lax.ppermute(x, axis, [(i, i ^ 1 << distance) for i in range(lax.axis_size(axis))])


def slot_index(route_block, expert_count, capacity):
    flat_routes = route_block.reshape(-1)
    labels = jnp.arange(2 * expert_count, dtype=jnp.int32)
    one_hot = (flat_routes[:, None] == labels[None, :]).astype(jnp.int32)
    earlier = jnp.sum((jnp.cumsum(one_hot, axis=0) - 1) * one_hot, axis=1)
    host = flat_routes % expert_count
    kind = flat_routes // expert_count
    return (host * 2 + kind) * capacity + earlier


def expert_pass(rows_x, rows_dh, w_one, w_two):
    gate_proj = jnp.dot(rows_x, w_one, preferred_element_type=jnp.float32)
    up_proj = jnp.dot(rows_x, w_two, preferred_element_type=jnp.float32)
    sig_gate = jax.nn.sigmoid(gate_proj)
    cot_rows = rows_dh.astype(jnp.float32)
    d_gate = (cot_rows * up_proj * sig_gate * (1.0 + gate_proj * (1.0 - sig_gate))).astype(
        jnp.bfloat16
    )
    d_up = (cot_rows * gate_proj * sig_gate).astype(jnp.bfloat16)
    dims_back = (((1,), (1,)), ((), ()))
    back_rows = (
        lax.dot_general(d_gate, w_one, dims_back, preferred_element_type=jnp.float32)
        + lax.dot_general(d_up, w_two, dims_back, preferred_element_type=jnp.float32)
    ).astype(jnp.bfloat16)
    dims_weight = (((0,), (0,)), ((), ()))
    part_gate = lax.dot_general(
        rows_x, d_gate, dims_weight, preferred_element_type=jnp.float32
    ).astype(jnp.bfloat16)
    part_up = lax.dot_general(rows_x, d_up, dims_weight, preferred_element_type=jnp.float32).astype(
        jnp.bfloat16
    )
    return (back_rows, part_gate, part_up)


def body(tokens, row_cotangent, routes, w_gate, w_up):
    expert_count = lax.axis_size("expert")
    token_count = tokens.shape[0]
    top_k = routes.shape[1]
    model_width = tokens.shape[1]
    hidden = w_gate.shape[2]
    capacity = 3 * token_count * top_k // (4 * expert_count)
    swap_bit = expert_count.bit_length() - 2
    position = slot_index(routes, expert_count, capacity)
    send_x = (
        jnp.zeros((expert_count * 2 * capacity, model_width), jnp.bfloat16)
        .at[position]
        .set(jnp.repeat(tokens, top_k, axis=0))
    )
    send_d = (
        jnp.zeros((expert_count * 2 * capacity, hidden), jnp.bfloat16)
        .at[position]
        .set(row_cotangent.reshape(-1, hidden))
    )
    recv_rows, recv_cots = (
        lax.all_to_all(
            send_x.reshape(expert_count, 2 * capacity, model_width),
            "expert",
            split_axis=0,
            concat_axis=0,
            tiled=True,
        ),
        lax.all_to_all(
            send_d.reshape(expert_count, 2 * capacity, hidden),
            "expert",
            split_axis=0,
            concat_axis=0,
            tiled=True,
        ),
    )
    home_x = recv_rows[:, :capacity].reshape(-1, model_width)
    home_d = recv_cots[:, :capacity].reshape(-1, hidden)
    copy_x = recv_rows[:, capacity:].reshape(-1, model_width)
    copy_d = recv_cots[:, capacity:].reshape(-1, hidden)
    own_gate = w_gate[0]
    own_up = w_up[0]
    home_back, home_pg, home_pu = expert_pass(home_x, home_d, own_gate, own_up)
    other_gate, other_up = partner((own_gate, own_up), "expert", swap_bit)
    copy_back, host_pg, host_pu = expert_pass(copy_x, copy_d, other_gate, other_up)
    copy_pg, copy_pu = partner((host_pg, host_pu), "expert", swap_bit)
    gate_terms = (home_pg.astype(jnp.float32) + copy_pg.astype(jnp.float32))[None]
    up_terms = (home_pu.astype(jnp.float32) + copy_pu.astype(jnp.float32))[None]
    back_all = jnp.concatenate(
        [
            home_back.reshape(expert_count, capacity, model_width),
            copy_back.reshape(expert_count, capacity, model_width),
        ],
        axis=1,
    )
    returned = lax.all_to_all(back_all, "expert", split_axis=0, concat_axis=0, tiled=True).reshape(
        -1, model_width
    )
    grad_tokens = returned[position].astype(jnp.float32).reshape(token_count, top_k, model_width)
    grad_tokens = grad_tokens.sum(axis=1).astype(jnp.bfloat16)
    shard_gate, shard_up = (
        lax.psum_scatter(
            gate_terms.astype(jnp.bfloat16), "dp", scatter_dimension=1, tiled=True
        ).astype(jnp.float32),
        lax.psum_scatter(
            up_terms.astype(jnp.bfloat16), "dp", scatter_dimension=1, tiled=True
        ).astype(jnp.float32),
    )
    total_gate = shard_gate[0]
    total_up = shard_up[0]
    replicas = lax.axis_size("dp")
    return (grad_tokens, (total_gate / replicas)[None], (total_up / replicas)[None])


def solution(mesh):
    return jax.shard_map(
        body,
        mesh=mesh,
        in_specs=(
            P(("dp", "expert"), None),
            P(("dp", "expert"), None, None),
            P(("dp", "expert"), None),
            P("expert", None, None),
            P("expert", None, None),
        ),
        out_specs=(P(("dp", "expert"), None), P("expert", "dp", None), P("expert", "dp", None)),
        check_vma=False,
    )
```

profile of v0, /device:TPU:1, one launch (start us, length us, event | category | flops | bytes accessed | tf_op | source)
XLA Modules:
  0.0 475.2 jit_solution(4403209228085323647)
XLA Ops:
  10.0 3.6 scatter_custom_fusion
  13.6 8.6 %all-to-all-start = ((bf16[32,24,768]{2,1,0:T(8,128)(2,1)}), bf16[32,24,768]{2,1,0:T(8,128)(2,1)}, u32[]{:S(2)}, u32[]{:S(2)}) async-start(bf16[32,24,768]{2,1,0:T(8,128)(2,1)} %bitcast.4), calls=%async_computation | async-start | bytes 2359296 | tf_op jit(solution)/shard_map/all_to_all | solution.py:72
  22.2 5.7 %scatter_custom_fusion.1 = bf16[768,2048]{1,0:T(8,128)(2,1)} fusion(s32[512]{0:T(512)S(1)} %bitcast.69, bf16[]{:T(256)} %constant.41.clone.1, bf16[64,2048]{1,0:T(8,128)(2,1)S(1)} %copy-done.8), kind=kCustom, calls=%fused_computation.15 | custom fusion | bytes 3407874 | tf_op jit(solution)/shard_map/scatter | solution.py:57
  27.9 12.0 %all-to-all-done = bf16[32,24,768]{2,1,0:T(8,128)(2,1)} async-done(((bf16[32,24,768]{2,1,0:T(8,128)(2,1)}), bf16[32,24,768]{2,1,0:T(8,128)(2,1)}, u32[]{:S(2)}, u32[]{:S(2)}) %all-to-all-start) | async-done | bytes 1179680 | tf_op jit(solution)/shard_map/all_to_all | solution.py:72
  39.9 5.3 %all-to-all-start.1 = ((bf16[32,24,2048]{2,1,0:T(8,128)(2,1)}), bf16[32,24,2048]{2,1,0:T(8,128)(2,1)S(1)}, u32[]{:S(2)}, u32[]{:S(2)}) async-start(bf16[32,24,2048]{2,1,0:T(8,128)(2,1)} %bitcast.66), calls=%async_computation.1 | async-start | bytes 6291456 | tf_op jit(solution)/shard_map/all_to_all | solution.py:65
  54.5 30.6 %all-to-all-done.1 = bf16[32,24,2048]{2,1,0:T(8,128)(2,1)S(1)} async-done(((bf16[32,24,2048]{2,1,0:T(8,128)(2,1)}), bf16[32,24,2048]{2,1,0:T(8,128)(2,1)S(1)}, u32[]{:S(2)}, u32[]{:S(2)}) %all-to-all-start.1) | async-done | bytes 3145760 | tf_op jit(solution)/shard_map/all_to_all | solution.py:65
  90.6 60.2 %collective-permute-done.1 = bf16[2048,768]{1,0:T(8,128)(2,1)} collective-permute-done((bf16[2048,768]{1,0:T(8,128)(2,1)}, bf16[2048,768]{1,0:T(8,128)(2,1)}, u32[]{:S(2)}, u32[]{:S(2)}) %collective-permute-start.1) | collective-permute-done | bytes 3145760 | tf_op jit(solution)/shard_map/ppermute | solution.py:8
  150.8 4.3 multiply_convert_fusion
  155.1 3.5 convolution_convert_fusion
  165.4 5.3 %multiply_convert_fusion.1 = (bf16[384,768]{1,0:T(8,128)(2,1)S(1)}, f32[384,768]{1,0:T(8,128)}) fusion(f32[384,768]{1,0:T(8,128)} %reshape.196, bf16[384,2048]{1,0:T(8,128)(2,1)} %reshape.191, bf16[1,2048,768]{2,1,0:T(8,128)(2,1)} %param.8), kind=kOutput, calls=%fused_computation.28 | convolution fusion | flops 1209729024 | bytes 7667712 | tf_op jit(solution)/shard_map/dot_general | solution.py:22
  170.7 58.5 %collective-permute-done.3 = bf16[2048,768]{1,0:T(8,128)(2,1)} collective-permute-done((bf16[2048,768]{1,0:T(8,128)(2,1)}, bf16[2048,768]{1,0:T(8,128)(2,1)}, u32[]{:S(2)}, u32[]{:S(2)}) %collective-permute-start.3) | collective-permute-done | bytes 3145760 | tf_op jit(solution)/shard_map/ppermute | solution.py:8
  229.2 5.4 %fusion.1 = bf16[1,2048,768]{2,1,0:T(8,128)(2,1)} fusion(bf16[2048,768]{1,0:T(8,128)(2,1)} %collective-permute-done.3, bf16[384,2048]{1,0:T(8,128)(2,1)S(1)} %copy-done.5, bf16[384,768]{1,0:T(8,128)(2,1)S(1)} %get-tuple-element.9), kind=kOutput, calls=%fused_computation.10 | convolution fusion | flops 1215823872 | bytes 8454144 | tf_op jit(solution)/shard_map/dot_general | solution.py:39
  234.7 61.9 %collective-permute-done = bf16[2048,768]{1,0:T(8,128)(2,1)} collective-permute-done((bf16[2048,768]{1,0:T(8,128)(2,1)}, bf16[2048,768]{1,0:T(8,128)(2,1)}, u32[]{:S(2)}, u32[]{:S(2)}) %collective-permute-start) | collective-permute-done | bytes 3145760 | tf_op jit(solution)/shard_map/ppermute | solution.py:8
  296.6 4.1 fusion.10
  307.1 65.1 %collective-permute-done.2 = bf16[2048,768]{1,0:T(8,128)(2,1)S(1)} collective-permute-done((bf16[2048,768]{1,0:T(8,128)(2,1)S(1)}, bf16[2048,768]{1,0:T(8,128)(2,1)S(1)}, u32[]{:S(2)}, u32[]{:S(2)}) %collective-permute-start.2) | collective-permute-done | bytes 3145760 | tf_op jit(solution)/shard_map/ppermute | solution.py:8
  372.2 3.6 fusion
  380.2 4.5 add_convert_fusion.3
  387.0 3.5 fusion.27
  390.6 4.5 add_convert_fusion.2
  395.1 3.6 reshape.194
  398.7 4.1 pad_maximum_fusion
  402.8 13.6 %all-to-all-start.2 = ((bf16[32,24,2048]{2,1,0:T(8,128)(2,1)}), bf16[32,24,2048]{2,1,0:T(8,128)(2,1)}, u32[]{:S(2)}, u32[]{:S(2)}) async-start(bf16[32,24,2048]{2,1,0:T(8,128)(2,1)} %pad_maximum_fusion), calls=%async_computation.2 | async-start | bytes 6291456 | tf_op jit(solution)/shard_map/all_to_all | solution.py:99
  416.5 39.1 %all-to-all-done.2 = bf16[32,24,2048]{2,1,0:T(8,128)(2,1)} async-done(((bf16[32,24,2048]{2,1,0:T(8,128)(2,1)}), bf16[32,24,2048]{2,1,0:T(8,128)(2,1)}, u32[]{:S(2)}, u32[]{:S(2)}) %all-to-all-start.2) | async-done | bytes 3145760 | tf_op jit(solution)/shard_map/all_to_all | solution.py:99
  455.6 6.8 %gather_fusion = bf16[512,2048]{1,0:T(8,128)(2,1)S(1)} fusion(bf16[768,2048]{1,0:T(8,128)(2,1)} %bitcast.9, s32[1024]{0:T(1024)S(1)} %pad_clamp_fusion), kind=kCustom, calls=%fused_computation | custom fusion | bytes 4196352 | tf_op jit(solution)/shard_map/gather | solution.py:102
  (69 shorter events, 43.5 us)
Async XLA Ops:
  7.2 2.8 copy-start
  10.0 12.2 %copy-start.8 = (bf16[64,2048]{1,0:T(8,128)(2,1)S(1)}, bf16[64,2048]{1,0:T(8,128)(2,1)}, u32[]{:S(2)}) copy-start(bf16[64,2048]{1,0:T(8,128)(2,1)} %param.5) | copy-start | bytes 786436
  13.6 26.4 %all-to-all-start = ((bf16[32,24,768]{2,1,0:T(8,128)(2,1)}), bf16[32,24,768]{2,1,0:T(8,128)(2,1)}, u32[]{:S(2)}, u32[]{:S(2)}) async-start(bf16[32,24,768]{2,1,0:T(8,128)(2,1)} %bitcast.4), calls=%async_computation | async-start | bytes 2359296 | tf_op jit(solution)/shard_map/all_to_all | solution.py:72
  39.9 45.1 %all-to-all-start.1 = ((bf16[32,24,2048]{2,1,0:T(8,128)(2,1)}), bf16[32,24,2048]{2,1,0:T(8,128)(2,1)S(1)}, u32[]{:S(2)}, u32[]{:S(2)}) async-start(bf16[32,24,2048]{2,1,0:T(8,128)(2,1)} %bitcast.66), calls=%async_computation.1 | async-start | bytes 6291456 | tf_op jit(solution)/shard_map/all_to_all | solution.py:65
  45.2 419.3 %reduce-scatter.5.cloned.1.call-start = ((), (), s32[]{:S(2)}) async-start(), calls=%async_computation.6 | async-start | bytes 3538944 | tf_op jit(solution)/shard_map/reduce_scatter | solution.py:108
  45.3 105.5 %collective-permute-start.1 = (bf16[2048,768]{1,0:T(8,128)(2,1)}, bf16[2048,768]{1,0:T(8,128)(2,1)}, u32[]{:S(2)}, u32[]{:S(2)}) collective-permute-start(bf16[2048,768]{1,0:T(8,128)(2,1)} %bitcast.71), channel_id=1, source_target_pairs={{0,16},{1,17},{2,18},{3,19},{4,20},{5,21},{6,22},{7,23},{8,24},{9,... | collective-permute-start | bytes 9437192 | tf_op jit(solution)/shard_map/ppermute | solution.py:8
  88.0 62.8 %copy-start.6 = (f32[384,768]{1,0:T(8,128)S(1)}, f32[384,768]{1,0:T(8,128)}, u32[]{:S(2)}) copy-start(f32[384,768]{1,0:T(8,128)} %reshape.197) | copy-start | bytes 3538948
  90.6 64.6 %copy-start.3 = (bf16[384,2048]{1,0:T(8,128)(2,1)}, bf16[384,2048]{1,0:T(8,128)(2,1)S(1)}, u32[]{:S(2)}) copy-start(bf16[384,2048]{1,0:T(8,128)(2,1)S(1)} %reshape.193) | copy-start | bytes 4718596
  155.1 3.5 copy-start.14
  158.6 5.4 %copy-start.2 = (bf16[32,12,2048]{2,1,0:T(8,128)(2,1)S(1)}, bf16[32,12,2048]{2,1,0:T(8,128)(2,1)}, u32[]{:S(2)}) copy-start(bf16[32,12,2048]{2,1,0:T(8,128)(2,1)} %get-tuple-element.3) | copy-start | bytes 4718596
  158.7 70.5 %collective-permute-start.3 = (bf16[2048,768]{1,0:T(8,128)(2,1)}, bf16[2048,768]{1,0:T(8,128)(2,1)}, u32[]{:S(2)}, u32[]{:S(2)}) collective-permute-start(bf16[2048,768]{1,0:T(8,128)(2,1)} %convolution_convert_fusion), channel_id=1, source_target_pairs={{0,16},{1,17},{2,18},{3,19},{4,20},{5,21},{6,22},{7,23},{8,24},{9,... | collective-permute-start | bytes 9437192 | tf_op jit(solution)/shard_map/ppermute | solution.py:8
  159.3 137.3 %collective-permute-start = (bf16[2048,768]{1,0:T(8,128)(2,1)}, bf16[2048,768]{1,0:T(8,128)(2,1)}, u32[]{:S(2)}, u32[]{:S(2)}) collective-permute-start(bf16[2048,768]{1,0:T(8,128)(2,1)} %bitcast.7), channel_id=1, source_target_pairs={{0,16},{1,17},{2,18},{3,19},{4,20},{5,21},{6,22},{7,23},{8,24},{9,... | collective-permute-start | bytes 9437192 | tf_op jit(solution)/shard_map/ppermute | solution.py:8
  165.4 63.8 %copy-start.5 = (bf16[384,2048]{1,0:T(8,128)(2,1)S(1)}, bf16[384,2048]{1,0:T(8,128)(2,1)}, u32[]{:S(2)}) copy-start(bf16[384,2048]{1,0:T(8,128)(2,1)} %reshape.191) | copy-start | bytes 4718596
  170.7 58.5 %copy-start.10 = (bf16[384,768]{1,0:T(8,128)(2,1)}, bf16[384,768]{1,0:T(8,128)(2,1)S(1)}, u32[]{:S(2)}) copy-start(bf16[384,768]{1,0:T(8,128)(2,1)S(1)} %get-tuple-element.9) | copy-start | bytes 1769476
  234.6 62.0 %copy-start.4 = (bf16[384,2048]{1,0:T(8,128)(2,1)S(1)}, bf16[384,2048]{1,0:T(8,128)(2,1)}, u32[]{:S(2)}) copy-start(bf16[384,2048]{1,0:T(8,128)(2,1)} %copy-done.3) | copy-start | bytes 4718596
  234.6 231.8 %reduce-scatter.3.cloned.1.call-start = ((), (), s32[]{:S(2)}) async-start(), calls=%async_computation.5 | async-start | bytes 3538944 | tf_op jit(solution)/shard_map/reduce_scatter | solution.py:105
  300.7 2.9 copy-start.7
  300.7 2.9 copy-start.16
  302.6 69.6 %collective-permute-start.2 = (bf16[2048,768]{1,0:T(8,128)(2,1)S(1)}, bf16[2048,768]{1,0:T(8,128)(2,1)S(1)}, u32[]{:S(2)}, u32[]{:S(2)}) collective-permute-start(bf16[2048,768]{1,0:T(8,128)(2,1)S(1)} %convolution_convert_fusion.2), channel_id=1, source_target_pairs={{0,16},{1,17},{2,18},{3,19},{4,20},{5,21},{6,22},{7,23},{8,24},{9,... | collective-permute-start | bytes 9437192 | tf_op jit(solution)/shard_map/ppermute | solution.py:8
  307.1 65.1 %copy-start.15 = (bf16[384,768]{1,0:T(8,128)(2,1)}, bf16[384,768]{1,0:T(8,128)(2,1)S(1)}, u32[]{:S(2)}) copy-start(bf16[384,768]{1,0:T(8,128)(2,1)S(1)} %fusion.9) | copy-start | bytes 1769476
  377.6 2.5 copy-start.11
  387.0 3.6 copy-start.13
  402.8 52.7 %all-to-all-start.2 = ((bf16[32,24,2048]{2,1,0:T(8,128)(2,1)}), bf16[32,24,2048]{2,1,0:T(8,128)(2,1)}, u32[]{:S(2)}, u32[]{:S(2)}) async-start(bf16[32,24,2048]{2,1,0:T(8,128)(2,1)} %pad_maximum_fusion), calls=%async_computation.2 | async-start | bytes 6291456 | tf_op jit(solution)/shard_map/all_to_all | solution.py:99
  455.6 12.8 %copy-start.1 = (bf16[64,8,768]{2,1,0:T(8,128)(2,1)S(1)}, bf16[64,8,768]{2,1,0:T(8,128)(2,1)}, u32[]{:S(2)}) copy-start(bf16[64,8,768]{2,1,0:T(8,128)(2,1)} %param.6) | copy-start | bytes 2359300
  (2 other events, 3.8 us)
Sparse Core Ops, SparseCore 0:
  234.7 52.4 reduce-scatter.4
  375.9 52.8 reduce-scatter.2
where the time goes:
time: 478 us; the launch traced here: 475 us
  waiting for transfers between devices  327 us (68%)
  matrix products  46.5 us (10%)
  local copies, waits for them, and re-layouts  37 us (8%)
  starting transfers between devices  34.9 us (7%)
  other arithmetic  15 us (3%)
  between operations  14.3 us (3%)
    ppermute x4, waiting for transfers between devices, partner(): lax.ppermute(x, axis, [(i, i ^ 1 << distance) for i in range(lax.axis_siz...  246 us
    all_to_all x1, waiting for transfers between devices, body(): lax.all_to_all(back_all, 'expert', split_axis=0, concat_axis=0, tiled=True)  39.1 us
    all_to_all x1, waiting for transfers between devices, body(): lax.all_to_all(send_x.reshape(expert_count, 2 * capacity, model_width), '...  30.6 us
    all_to_all x1, starting transfers between devices, body(): lax.all_to_all(back_all, 'expert', split_axis=0, concat_axis=0, tiled=True)  13.6 us
    all_to_all x1, waiting for transfers between devices, body(): lax.all_to_all(send_d.reshape(expert_count, 2 * capacity, hidden), 'exper...  12 us
    dot_general x2, matrix products, expert_pass(): gate_proj = jnp.dot(rows_x, w_one, preferred_element_type=jnp.float32)  9.6 us
  transfers between devices with their start and end apart: 9, of which 7 were waited for; matrix products, arithmetic and copies ran while one was open for 17% of the time, Pallas kernels for 0%

commit v1 on v0

--- a/solution.py
+++ b/solution.py
@@ -2,10 +2,6 @@
 import jax.numpy as jnp
 from jax import lax
 from jax.sharding import PartitionSpec as P
-
-
-def partner(x, axis, distance):
-    return lax.ppermute(x, axis, [(i, i ^ 1 << distance) for i in range(lax.axis_size(axis))])
 
 
 def slot_index(route_block, expert_count, capacity):
@@ -13,9 +9,9 @@
     labels = jnp.arange(2 * expert_count, dtype=jnp.int32)
     one_hot = (flat_routes[:, None] == labels[None, :]).astype(jnp.int32)
     earlier = jnp.sum((jnp.cumsum(one_hot, axis=0) - 1) * one_hot, axis=1)
-    host = flat_routes % expert_count
     kind = flat_routes // expert_count
-    return (host * 2 + kind) * capacity + earlier
+    home = jnp.bitwise_xor(flat_routes % expert_count, kind * (expert_count // 2))
+    return (home * 2 + kind) * capacity + earlier
 
 
 def expert_pass(rows_x, rows_dh, w_one, w_two):
@@ -49,7 +45,6 @@
     model_width = tokens.shape[1]
     hidden = w_gate.shape[2]
     capacity = 3 * token_count * top_k // (4 * expert_count)
-    swap_bit = expert_count.bit_length() - 2
     position = slot_index(routes, expert_count, capacity)
     send_x = (
         jnp.zeros((expert_count * 2 * capacity, model_width), jnp.bfloat16)
@@ -77,25 +72,11 @@
             tiled=True,
         ),
     )
-    home_x = recv_rows[:, :capacity].reshape(-1, model_width)
-    home_d = recv_cots[:, :capacity].reshape(-1, hidden)
-    copy_x = recv_rows[:, capacity:].reshape(-1, model_width)
-    copy_d = recv_cots[:, capacity:].reshape(-1, hidden)
-    own_gate = w_gate[0]
-    own_up = w_up[0]
-    home_back, home_pg, home_pu = expert_pass(home_x, home_d, own_gate, own_up)
-    other_gate, other_up = partner((own_gate, own_up), "expert", swap_bit)
-    copy_back, host_pg, host_pu = expert_pass(copy_x, copy_d, other_gate, other_up)
-    copy_pg, copy_pu = partner((host_pg, host_pu), "expert", swap_bit)
-    gate_terms = (home_pg.astype(jnp.float32) + copy_pg.astype(jnp.float32))[None]
-    up_terms = (home_pu.astype(jnp.float32) + copy_pu.astype(jnp.float32))[None]
-    back_all = jnp.concatenate(
-        [
-            home_back.reshape(expert_count, capacity, model_width),
-            copy_back.reshape(expert_count, capacity, model_width),
-        ],
-        axis=1,
+    back_all, gate_terms, up_terms = expert_pass(
+        recv_rows.reshape(-1, model_width), recv_cots.reshape(-1, hidden), w_gate[0], w_up[0]
     )
+    back_all = back_all.reshape(expert_count, 2 * capacity, model_width)
+    gate_terms, up_terms = gate_terms[None], up_terms[None]
     returned = lax.all_to_all(back_all, "expert", split_axis=0, concat_axis=0, tiled=True).reshape(
         -1, model_width
     )
@@ -103,10 +84,10 @@
     grad_tokens = grad_tokens.sum(axis=1).astype(jnp.bfloat16)
     shard_gate, shard_up = (
         lax.psum_scatter(
-            gate_terms.astype(jnp.bfloat16), "dp", scatter_dimension=1, tiled=True
+            gate_terms, "dp", scatter_dimension=1, tiled=True
         ).astype(jnp.float32),
         lax.psum_scatter(
-            up_terms.astype(jnp.bfloat16), "dp", scatter_dimension=1, tiled=True
+            up_terms, "dp", scatter_dimension=1, tiled=True
         ).astype(jnp.float32),
     )
     total_gate = shard_gate[0]

time: 478 us -> 205 us (0.43)
  waiting for transfers between devices: 327 us -> 71.2 us
  blocking collectives: 0 us -> 45 us
  starting transfers between devices: 34.9 us -> 13.7 us
  matrix products: 46.5 us -> 29.3 us
  local copies, waits for them, and re-layouts: 37 us -> 20 us
  other arithmetic: 15 us -> 9.02 us
    ppermute x4 -> x0, waiting for transfers between devices: 246 us -> none  [partner(): lax.ppermute(x, axis, [(i, i ^ 1 << distance) for i in range(lax.axis_siz...]
    all_to_all x0 -> x1, blocking collectives: none -> 45 us  [body(): lax.all_to_all(send_x.reshape(expert_count, 2 * capacity, model_width), '...]
    all_to_all x1 -> x0, waiting for transfers between devices: 30.6 us -> none  [body(): lax.all_to_all(send_x.reshape(expert_count, 2 * capacity, model_width), '...]
    reduce_scatter x2, waiting for transfers between devices: 0.01 us -> 19.9 us  [the longest x1 19.9 us: body(): lax.psum_scatter(up_terms, 'dp', scatter_dimension=1, tiled=True)]
    reshape x4 -> x0, local copies, waits for them, and re-layouts: 9.94 us -> none  [the longest x1 3.64 us: body(): copy_back.reshape(expert_count, capacity, model_width)]
    all_to_all x1, starting transfers between devices: 13.6 us -> 5.02 us  [body(): lax.all_to_all(back_all, 'expert', split_axis=0, concat_axis=0, tiled=True)]
    ppermute x4 -> x0, starting transfers between devices: 7.27 us -> none  [partner(): lax.ppermute(x, axis, [(i, i ^ 1 << distance) for i in range(lax.axis_siz...]
    all_to_all x1 -> x0, starting transfers between devices: 5.28 us -> none  [body(): lax.all_to_all(send_x.reshape(expert_count, 2 * capacity, model_width), '...]
  transfers between devices with their start and end apart: 9 -> 4, of which waited for: 7 -> 3; matrix products, arithmetic and copies ran while one was open for 17% -> 17% of each run, Pallas kernels for 0% -> 0%
where the time goes in v1:
time: 205 us; the launch traced here: 202 us
  waiting for transfers between devices  71.2 us (35%)
  blocking collectives  45 us (22%)
  matrix products  29.3 us (14%)
  local copies, waits for them, and re-layouts  20 us (10%)
  between operations  14.2 us (7%)
  starting transfers between devices  13.7 us (7%)
  other arithmetic  9.02 us (4%)
    all_to_all x1, blocking collectives, body(): lax.all_to_all(send_x.reshape(expert_count, 2 * capacity, model_width), '...  45 us
    all_to_all x1, waiting for transfers between devices, body(): lax.all_to_all(back_all, 'expert', split_axis=0, concat_axis=0, tiled=True)  39.3 us
    reduce_scatter x1, waiting for transfers between devices, body(): lax.psum_scatter(up_terms, 'dp', scatter_dimension=1, tiled=True)  19.9 us
    all_to_all x1, waiting for transfers between devices, body(): lax.all_to_all(send_d.reshape(expert_count, 2 * capacity, hidden), 'exper...  12 us
    all_to_all x1, starting transfers between devices, body(): lax.all_to_all(send_d.reshape(expert_count, 2 * capacity, hidden), 'exper...  8.64 us
    gather x1, local copies, waits for them, and re-layouts, body(): returned[position].astype(jnp.float32)  7.69 us
    dot_general x1, matrix products, expert_pass(): lax.dot_general(rows_x, d_up, dims_weight, preferred_element_type=jnp.flo...  6.6 us
    dot_general x1, matrix products, expert_pass(): gate_proj = jnp.dot(rows_x, w_one, preferred_element_type=jnp.float32)  6.17 us
  transfers between devices with their start and end apart: 4, of which 3 were waited for; matrix products, arithmetic and copies ran while one was open for 17% of the time, Pallas kernels for 0%

profile of v1, /device:TPU:1, one launch (start us, length us, event | category | flops | bytes accessed | tf_op | source)
XLA Modules:
  0.0 202.5 jit_solution(13148397568121845332)
XLA Ops:
  7.2 0.9 copy.8
  8.1 0.1 eq.31
  8.4 1.2 reduce-window.6
  9.6 0.2 slice_reduce_fusion
  9.9 0.1 fusion.24
  10.0 4.2 %scatter_custom_fusion = bf16[768,768]{1,0:T(8,128)(2,1)} fusion(s32[512]{0:T(512)S(1)} %bitcast.69, bf16[64,8,768]{2,1,0:T(8,128)(2,1)} %param.6, bf16[]{:T(256)} %constant.42.clone.1), kind=kCustom, calls=%fused_computation.28 | custom fusion | bytes 1966082 | tf_op jit(solution)/shard_map/scatter | solution.py:57
  14.2 8.6 %all-to-all-start = ((bf16[32,24,768]{2,1,0:T(8,128)(2,1)}), bf16[32,24,768]{2,1,0:T(8,128)(2,1)}, u32[]{:S(2)}, u32[]{:S(2)}) async-start(bf16[32,24,768]{2,1,0:T(8,128)(2,1)} %bitcast.62), calls=%async_computation | async-start | bytes 2359296 | tf_op jit(solution)/shard_map/all_to_all | solution.py:67
  22.9 5.7 %scatter_custom_fusion.1 = bf16[768,2048]{1,0:T(8,128)(2,1)} fusion(s32[512]{0:T(512)S(1)} %bitcast.70, bf16[]{:T(256)} %constant.42.clone.1, bf16[64,2048]{1,0:T(8,128)(2,1)S(1)} %copy-done.2), kind=kCustom, calls=%fused_computation.24 | custom fusion | bytes 3407874 | tf_op jit(solution)/shard_map/scatter | solution.py:52
  28.6 12.0 %all-to-all-done = bf16[32,24,768]{2,1,0:T(8,128)(2,1)} async-done(((bf16[32,24,768]{2,1,0:T(8,128)(2,1)}), bf16[32,24,768]{2,1,0:T(8,128)(2,1)}, u32[]{:S(2)}, u32[]{:S(2)}) %all-to-all-start) | async-done | bytes 1179680 | tf_op jit(solution)/shard_map/all_to_all | solution.py:67
  40.6 45.0 %all_to_all.15 = bf16[32,24,2048]{2,1,0:T(8,128)(2,1)S(1)} all-to-all(bf16[32,24,2048]{2,1,0:T(8,128)(2,1)} %bitcast.61), channel_id=1, replica_groups=mesh['dp'=8,'expert'=32] {'expert'}, dimensions={0} | all-to-all | bytes 6291456 | tf_op jit(solution)/shard_map/all_to_all | solution.py:60
  85.6 6.2 %fusion.13 = (bf16[768,768]{1,0:T(8,128)(2,1)}, f32[768,768]{1,0:T(8,128)S(1)}) fusion(bf16[32,24,768]{2,1,0:T(8,128)(2,1)} %all-to-all-done, bf16[768,2048]{1,0:T(8,128)(2,1)S(1)} %bitcast.63, bf16[1,2048,768]{2,1,0:T(8,128)(2,1)S(1)} %copy-done), kind=kOutput, calls=%fused_computation.21 | convolution fusion | flops 2420047872 | bytes 11010048 | tf_op jit(solution)/shard_map/dot_general | solution.py:18
  91.8 4.4 %fusion.11 = bf16[768,768]{1,0:T(8,128)(2,1)S(1)} fusion(bf16[768,768]{1,0:T(8,128)(2,1)} %bitcast.11, f32[768,768]{1,0:T(8,128)S(1)} %get-tuple-element.4, bf16[768,2048]{1,0:T(8,128)(2,1)S(1)} %bitcast.64, bf16[1,2048,768]{2,1,0:T(8,128)(2,1)S(1)} %copy-done.3), kind=kOutput, calls=%fused_computation.19 | convolution fusion | flops 2422407168 | bytes 11010048 | tf_op jit(solution)/shard_map/dot_general | solution.py:19
  96.2 1.0 copy-done.5
  97.2 4.1 %fusion.7 = bf16[1,2048,768]{2,1,0:T(8,128)(2,1)} fusion(bf16[768,2048]{1,0:T(8,128)(2,1)S(1)} %bitcast.65, bf16[768,768]{1,0:T(8,128)(2,1)S(1)} %fusion.11), kind=kOutput, calls=%fused_computation.13 | convolution fusion | flops 2417491968 | bytes 7471104 | tf_op jit(solution)/shard_map/dot_general | solution.py:32
  101.3 6.6 %fusion.8 = bf16[1,2048,768]{2,1,0:T(8,128)(2,1)} fusion(bf16[768,2048]{1,0:T(8,128)(2,1)} %bitcast.66, bf16[768,768]{1,0:T(8,128)(2,1)} %get-tuple-element.3), kind=kOutput, calls=%fused_computation.14 | convolution fusion | flops 2417491968 | bytes 7471104 | tf_op jit(solution)/shard_map/dot_general | solution.py:35
  108.0 4.0 %fusion = f32[768,2048]{1,0:T(8,128)S(1)} fusion(bf16[768,768]{1,0:T(8,128)(2,1)} %copy-done.5, bf16[1,2048,768]{2,1,0:T(8,128)(2,1)S(1)} %copy-done), kind=kOutput, calls=%fused_computation.6 | convolution fusion | flops 2415919104 | bytes 10616832 | tf_op jit(solution)/shard_map/dot_general | solution.py:28
  112.0 4.0 %add_convert_fusion = bf16[768,2048]{1,0:T(8,128)(2,1)} fusion(f32[768,2048]{1,0:T(8,128)S(1)} %fusion, bf16[768,768]{1,0:T(8,128)(2,1)S(1)} %copy-done.6, bf16[1,2048,768]{2,1,0:T(8,128)(2,1)S(1)} %copy-done.4), kind=kOutput, calls=%fused_computation.3 | convolution fusion | flops 2419064832 | bytes 13762560 | tf_op jit(solution)/shard_map/dot_general | solution.py:29
  116.1 5.0 %all-to-all-start.2 = ((bf16[32,24,2048]{2,1,0:T(8,128)(2,1)}), bf16[32,24,2048]{2,1,0:T(8,128)(2,1)}, u32[]{:S(2)}, u32[]{:S(2)}) async-start(bf16[32,24,2048]{2,1,0:T(8,128)(2,1)} %bitcast.67), calls=%async_computation.2 | async-start | bytes 6291456 | tf_op jit(solution)/shard_map/all_to_all | solution.py:80
  121.1 39.3 %all-to-all-done.2 = bf16[32,24,2048]{2,1,0:T(8,128)(2,1)} async-done(((bf16[32,24,2048]{2,1,0:T(8,128)(2,1)}), bf16[32,24,2048]{2,1,0:T(8,128)(2,1)}, u32[]{:S(2)}, u32[]{:S(2)}) %all-to-all-start.2) | async-done | bytes 3145760 | tf_op jit(solution)/shard_map/all_to_all | solution.py:80
  160.4 7.7 %gather_fusion = bf16[512,2048]{1,0:T(8,128)(2,1)} fusion(bf16[768,2048]{1,0:T(8,128)(2,1)} %bitcast.13, s32[1024]{0:T(1024)S(1)} %pad_clamp_fusion), kind=kCustom, calls=%fused_computation | custom fusion | bytes 4196352 | tf_op jit(solution)/shard_map/gather | solution.py:83
  168.1 3.7 %bitcast_reduce_fusion = bf16[64,2048]{1,0:T(8,128)(2,1)} fusion(bf16[512,2048]{1,0:T(8,128)(2,1)} %gather_fusion), kind=kLoop, calls=%fused_computation.23 | loop fusion | flops 917504 | bytes 2359296 | tf_op jit(solution)/shard_map/reduce_sum | solution.py:84
  171.9 1.9 convert_multiply_fusion.3
  173.8 19.9 %reduce-scatter.5.cloned.1.call-done = bf16[1,256,768]{2,1,0:T(8,128)(2,1)} async-done(((bf16[1,2048,768]{2,1,0:T(8,128)(2,1)}), bf16[1,256,768]{2,1,0:T(8,128)(2,1)}) %reduce-scatter.5.cloned.1.call-update) | async-done | bytes 393232 | tf_op jit(solution)/shard_map/reduce_scatter | solution.py:89
  193.7 1.9 convert_multiply_fusion.2
  (25 shorter events, 0.4 us)
Async XLA Ops:
  7.2 78.5 %copy-start = (bf16[1,2048,768]{2,1,0:T(8,128)(2,1)S(1)}, bf16[1,2048,768]{2,1,0:T(8,128)(2,1)}, u32[]{:S(2)}) copy-start(bf16[1,2048,768]{2,1,0:T(8,128)(2,1)} %param.8) | copy-start | bytes 9437188
  9.6 13.3 %copy-start.2 = (bf16[64,2048]{1,0:T(8,128)(2,1)S(1)}, bf16[64,2048]{1,0:T(8,128)(2,1)}, u32[]{:S(2)}) copy-start(bf16[64,2048]{1,0:T(8,128)(2,1)} %param.5) | copy-start | bytes 786436
  14.2 26.4 %all-to-all-start = ((bf16[32,24,768]{2,1,0:T(8,128)(2,1)}), bf16[32,24,768]{2,1,0:T(8,128)(2,1)}, u32[]{:S(2)}, u32[]{:S(2)}) async-start(bf16[32,24,768]{2,1,0:T(8,128)(2,1)} %bitcast.62), calls=%async_computation | async-start | bytes 2359296 | tf_op jit(solution)/shard_map/all_to_all | solution.py:67
  22.8 149.0 %reduce-scatter.3.cloned.1.call-start = ((), (), s32[]{:S(2)}) async-start(), calls=%async_computation.5 | async-start | bytes 3538944 | tf_op jit(solution)/shard_map/reduce_scatter | solution.py:86
  85.6 10.5 %copy-start.1 = (bf16[32,24,2048]{2,1,0:T(8,128)(2,1)}, bf16[32,24,2048]{2,1,0:T(8,128)(2,1)S(1)}, u32[]{:S(2)}) copy-start(bf16[32,24,2048]{2,1,0:T(8,128)(2,1)S(1)} %all_to_all.15) | copy-start | bytes 9437188
  85.6 6.2 %copy-start.3 = (bf16[1,2048,768]{2,1,0:T(8,128)(2,1)S(1)}, bf16[1,2048,768]{2,1,0:T(8,128)(2,1)}, u32[]{:S(2)}) copy-start(bf16[1,2048,768]{2,1,0:T(8,128)(2,1)} %param.9) | copy-start | bytes 9437188
  96.2 1.0 copy-start.5
  101.3 92.4 %reduce-scatter.5.cloned.1.call-start = ((), (), s32[]{:S(2)}) async-start(), calls=%async_computation.6 | async-start | bytes 3538944 | tf_op jit(solution)/shard_map/reduce_scatter | solution.py:89
  108.0 4.1 %copy-start.4 = (bf16[1,2048,768]{2,1,0:T(8,128)(2,1)S(1)}, bf16[1,2048,768]{2,1,0:T(8,128)(2,1)}, u32[]{:S(2)}) copy-start(bf16[1,2048,768]{2,1,0:T(8,128)(2,1)} %param.9) | copy-start | bytes 9437188
  108.0 4.1 %copy-start.6 = (bf16[768,768]{1,0:T(8,128)(2,1)S(1)}, bf16[768,768]{1,0:T(8,128)(2,1)}, u32[]{:S(2)}) copy-start(bf16[768,768]{1,0:T(8,128)(2,1)} %get-tuple-element.3) | copy-start | bytes 3538948
  116.1 44.3 %all-to-all-start.2 = ((bf16[32,24,2048]{2,1,0:T(8,128)(2,1)}), bf16[32,24,2048]{2,1,0:T(8,128)(2,1)}, u32[]{:S(2)}, u32[]{:S(2)}) async-start(bf16[32,24,2048]{2,1,0:T(8,128)(2,1)} %bitcast.67), calls=%async_computation.2 | async-start | bytes 6291456 | tf_op jit(solution)/shard_map/all_to_all | solution.py:80
Sparse Core Ops, SparseCore 0:
  101.4 43.6 reduce-scatter.2
  147.6 46.0 reduce-scatter.4

commit v2 on v1

v2 whole, which is shorter than its diff:
```python
import functools

import jax
import jax.numpy as jnp
from jax import lax
from jax.experimental import pallas as pl
from jax.experimental.pallas import tpu as pltpu
from jax.sharding import PartitionSpec as P

MESH = pl.DeviceIdType.MESH
F32, BF16 = jnp.float32, jnp.bfloat16


def slot_index(route_block, expert_count, capacity):
    flat_routes = route_block.reshape(-1)
    labels = jnp.arange(2 * expert_count, dtype=jnp.int32)
    one_hot = (flat_routes[:, None] == labels[None, :]).astype(jnp.int32)
    earlier = jnp.sum((jnp.cumsum(one_hot, axis=0) - 1) * one_hot, axis=1)
    kind = flat_routes // expert_count
    home = jnp.bitwise_xor(flat_routes % expert_count, kind * (expert_count // 2))
    return (home * 2 + kind) * capacity + earlier


def expert_kernel(
    dims,
    xs_ref, dh_ref, pos_ref, wg_hbm, wu_hbm,
    gt_ref, gg_ref, gu_ref,
    w_ref, d_ref, ring_ref, part_ref, back_ref, ret_ref, comb_ref,
    w_sem, ring_send, ring_recv, ret_send, ret_recv, own_sem,
):
    n_dp, n_ex, slots, tok, top = dims
    width, hidden = w_ref.shape[1], w_ref.shape[2]
    rows = xs_ref.shape[0]
    cols = width // n_dp
    half = cols // 2
    me = lax.axis_index("expert")
    p = lax.axis_index("dp")
    w_copies = [
        pltpu.make_async_copy(src, w_ref.at[k], w_sem.at[k])
        for k, src in enumerate((wg_hbm, wu_hbm))
    ]
    for c in w_copies:
        c.start()
    barrier = pltpu.get_barrier_semaphore()
    right, left = lax.rem(p + 1, n_dp), lax.rem(p + n_dp - 1, n_dp)
    for z in (left, right):
        pl.semaphore_signal(barrier, inc=1, device_id={"dp": z}, device_id_type=MESH)

    def greet(k, c):
        pl.semaphore_signal(
            barrier, inc=1, device_id={"expert": lax.rem(me + k, n_ex)}, device_id_type=MESH
        )
        return c

    lax.fori_loop(1, n_ex, greet, 0)

    wide = 2 * n_ex * slots
    place = lax.broadcasted_iota(jnp.int32, (tok * top, wide), 1)
    row_of = lax.broadcasted_iota(jnp.int32, (tok, tok * top), 1)
    token_of = lax.broadcasted_iota(jnp.int32, (tok, tok * top), 0) * top
    group = jnp.where((row_of >= token_of) & (row_of < token_of + top), 1.0, 0.0).astype(BF16)
    for k in range(2):
        hit = jnp.where(place == pos_ref[...] + k * slots, 1.0, 0.0).astype(BF16)
        comb_ref[k * tok:(k + 1) * tok, :] = jnp.dot(
            group, hit, preferred_element_type=F32
        ).astype(BF16)

    for c in w_copies:
        c.wait()
    m_blk, n_blk = rows // 2, 256

    def gates(i, c):
        r = pl.ds(pl.multiple_of(i * m_blk, m_blk), m_blk)
        for n in range(hidden // n_blk):
            cs = slice(n * n_blk, (n + 1) * n_blk)
            g = jnp.dot(xs_ref[r, :], w_ref[0, :, cs], preferred_element_type=F32)
            u = jnp.dot(xs_ref[r, :], w_ref[1, :, cs], preferred_element_type=F32)
            s = jax.nn.sigmoid(g)
            h = dh_ref[r, cs].astype(F32)
            d_ref[r, cs] = (h * u * s * (1.0 + g * (1.0 - s))).astype(BF16)
            d_ref[r, hidden + n * n_blk:hidden + (n + 1) * n_blk] = (h * g * s).astype(BF16)
        return c

    lax.fori_loop(0, 2, gates, 0)

    def part(c, k):
        x_cols = xs_ref[:, pl.ds(pl.multiple_of(c * cols, cols), cols)]
        return lax.dot_general(
            x_cols, d_ref[:, k * hidden:(k + 1) * hidden],
            (((0,), (0,)), ((), ())), preferred_element_type=F32,
        )

    def chunk(s, k):
        return lax.rem(p + n_dp - 1 - s, n_dp) if k == 0 else lax.rem(p + 1 + s, n_dp)

    def ring_copy(s, k, b):
        sl = pl.ds(b * half, half)
        return pltpu.make_async_remote_copy(
            src_ref=ring_ref.at[k, s, sl],
            dst_ref=ring_ref.at[k, s + 1, sl],
            send_sem=ring_send.at[k, s, b],
            recv_sem=ring_recv.at[k, s, b],
            device_id={"dp": right if k == 0 else left},
            device_id_type=MESH,
        )

    pl.semaphore_wait(barrier, n_ex + 1)
    for k in range(2):
        ring_ref[k, 0] = part(chunk(0, k), k).astype(BF16)
        for b in range(2):
            ring_copy(0, k, b).start()

    side = 8
    wide_col = width // 2

    def back_chunk(i):
        y = lax.rem(me // side + i, n_ex // side)
        r = pl.ds(pl.multiple_of(y * side * slots, side * slots), side * slots)
        for h in range(2):
            wc = slice(h * wide_col, (h + 1) * wide_col)
            dims_back = (((1,), (1,)), ((), ()))
            b = lax.dot_general(
                d_ref[r, :hidden], w_ref[0, wc, :], dims_back, preferred_element_type=F32
            ) + lax.dot_general(
                d_ref[r, hidden:], w_ref[1, wc, :], dims_back, preferred_element_type=F32
            )
            part_rows = b.reshape(side, slots, wide_col)
            for j in range(side):
                back_ref[y * side + j, h * slots:(h + 1) * slots, :] = part_rows[j].astype(BF16)
        return y

    def ret_copy(t):
        return pltpu.make_async_remote_copy(
            src_ref=back_ref.at[t],
            dst_ref=ret_ref.at[me],
            send_sem=ret_send.at[t],
            recv_sem=ret_recv.at[me],
            device_id={"expert": t},
            device_id_type=MESH,
        )

    own_copy = pltpu.make_async_copy(back_ref.at[me], ret_ref.at[me], own_sem)

    def start_returns(i, y):
        def go(j, c):
            ret_copy(y * side + lax.rem(me + j, side)).start()
            return c

        if i == 0:
            own_copy.start()
            lax.fori_loop(1, side, go, 0)
        else:
            lax.fori_loop(0, side, go, 0)

    def ring_step(s):
        for k in range(2):
            part_ref[k] = part(chunk(s, k), k)
        for b in range(2):
            sl = pl.ds(b * half, half)
            for k in range(2):
                ring_copy(s - 1, k, b).wait_recv()
                ring_ref[k, s, sl] = (
                    ring_ref[k, s, sl].astype(F32) + part_ref[k, sl]
                ).astype(BF16)
                ring_copy(s, k, b).start()

    start_returns(0, back_chunk(0))
    ring_step(1)

    def both(s, c):
        start_returns(1, back_chunk(s - 1))
        ring_step(s)
        return c

    lax.fori_loop(2, 5, both, 0)

    def alone(s, c):
        ring_step(s)
        return c

    lax.fori_loop(5, n_dp - 1, alone, 0)
    scale = 1.0 / n_dp
    for k in range(2):
        part_ref[k] = part(p, k)
    for b in range(2):
        sl = pl.ds(b * half, half)
        for k, out in enumerate((gg_ref, gu_ref)):
            ring_copy(n_dp - 2, k, b).wait_recv()
            out[sl] = (ring_ref[k, n_dp - 1, sl].astype(F32) + part_ref[k, sl]) * scale

    def got(j, c):
        t = lax.rem(me + j, n_ex)
        pltpu.make_async_remote_copy(
            src_ref=back_ref.at[t], dst_ref=ret_ref.at[t], send_sem=ret_send.at[t],
            recv_sem=ret_recv.at[t], device_id={"expert": t}, device_id_type=MESH,
        ).wait()
        return c

    lax.fori_loop(1, n_ex, got, 0)
    own_copy.wait()
    summed = jnp.dot(
        comb_ref[...], ret_ref[...].reshape(wide, wide_col), preferred_element_type=F32
    )
    gt_ref[:, :wide_col] = summed[:tok].astype(BF16)
    gt_ref[:, wide_col:] = summed[tok:].astype(BF16)

    def sent(s, c):
        for k in range(2):
            for b in range(2):
                ring_copy(s, k, b).wait_send()
        return c

    lax.fori_loop(0, n_dp - 1, sent, 0)


def body(tokens, row_cotangent, routes, w_gate, w_up):
    n_ex, n_dp = lax.axis_size("expert"), lax.axis_size("dp")
    tok, width = tokens.shape
    top = routes.shape[1]
    hidden = w_gate.shape[2]
    capacity = 3 * tok * top // (4 * n_ex)
    slots = 2 * capacity
    rows = n_ex * slots
    position = slot_index(routes, n_ex, capacity)
    send_x = (
        jnp.zeros((rows, width), BF16).at[position].set(jnp.repeat(tokens, top, axis=0))
    )
    send_d = jnp.zeros((rows, hidden), BF16).at[position].set(row_cotangent.reshape(-1, hidden))
    recv_x, recv_d = (
        lax.all_to_all(
            a.reshape(n_ex, slots, -1), "expert", split_axis=0, concat_axis=0, tiled=True
        ).reshape(rows, -1)
        for a in (send_x, send_d)
    )
    pos_col = (position // slots * (2 * slots) + position % slots)[:, None]
    vmem = pl.BlockSpec(memory_space=pltpu.VMEM)
    hbm = pl.BlockSpec(memory_space=pl.ANY)
    cols = width // n_dp
    dma = pltpu.SemaphoreType.DMA
    gt, gg, gu = pl.pallas_call(
        functools.partial(expert_kernel, (n_dp, n_ex, slots, tok, top)),
        out_shape=(
            jax.ShapeDtypeStruct((tok, width), BF16),
            jax.ShapeDtypeStruct((cols, hidden), F32),
            jax.ShapeDtypeStruct((cols, hidden), F32),
        ),
        in_specs=[vmem, vmem, vmem, hbm, hbm],
        out_specs=(vmem, vmem, vmem),
        scratch_shapes=[
            pltpu.VMEM((2, width, hidden), BF16),
            pltpu.VMEM((rows, 2 * hidden), BF16),
            pltpu.VMEM((2, n_dp, cols, hidden), BF16),
            pltpu.VMEM((2, cols, hidden), F32),
            pltpu.VMEM((n_ex, 2 * slots, width // 2), BF16),
            pltpu.VMEM((n_ex, 2 * slots, width // 2), BF16),
            pltpu.VMEM((2 * tok, 2 * rows), BF16),
            dma((2,)),
            dma((2, n_dp, 2)),
            dma((2, n_dp, 2)),
            dma((n_ex,)),
            dma((n_ex,)),
            dma,
        ],
        compiler_params=pltpu.CompilerParams(
            collective_id=0, has_side_effects=True, vmem_limit_bytes=56 << 20
        ),
        name="expert_backward",
    )(recv_x, recv_d, pos_col, w_gate[0], w_up[0])
    return gt, gg[None], gu[None]


def solution(mesh):
    return jax.shard_map(
        body,
        mesh=mesh,
        in_specs=(
            P(("dp", "expert"), None),
            P(("dp", "expert"), None, None),
            P(("dp", "expert"), None),
            P("expert", None, None),
            P("expert", None, None),
        ),
        out_specs=(P(("dp", "expert"), None), P("expert", "dp", None), P("expert", "dp", None)),
        check_vma=False,
    )
```

time: 205 us -> 166 us (0.81); the launches traced: 202 us -> 166 us
  Pallas kernels: 0 us -> 80.2 us
  waiting for transfers between devices: 71.2 us -> 12 us
  matrix products: 29.3 us -> 0 us
  between operations: 14.2 us -> 0.72 us
  other arithmetic: 9.02 us -> 2.77 us
  starting transfers between devices: 13.7 us -> 8.59 us
  local copies, waits for them, and re-layouts: 20 us -> 15.5 us
    pallas_call x0 -> x1, Pallas kernels: none -> 80.2 us  [body(): pl.pallas_call(functools.partial(expert_kernel, (n_dp, n_ex, slots, tok,...]
    all_to_all x2 -> x1, waiting for transfers between devices: 51.3 us -> 12 us  [body(): lax.all_to_all(a.reshape(n_ex, slots, -1), 'expert', split_axis=0, concat...]
    dot_general x6 -> x0, matrix products: 29.3 us -> none  [the longest x1 6.6 us: expert_pass(): lax.dot_general(rows_x, d_up, dims_weight, preferred_element_type=jnp.flo...]
    reduce_scatter x2 -> x0, waiting for transfers between devices: 19.9 us -> none  [the longest x1 19.9 us: body(): lax.psum_scatter(up_terms, 'dp', scatter_dimension=1, tiled=True)]
    gather x1 -> x0, local copies, waits for them, and re-layouts: 7.69 us -> none  [body(): returned[position].astype(jnp.float32)]
    all_to_all x2 -> x1, starting transfers between devices: 13.7 us -> 8.59 us  [body(): lax.all_to_all(a.reshape(n_ex, slots, -1), 'expert', split_axis=0, concat...]
    div x2 -> x0, other arithmetic: 3.86 us -> none  [the longest x1 1.93 us: body(): total_gate / replicas]
    reduce_sum x1 -> x0, other arithmetic: 3.75 us -> none  [body(): grad_tokens = grad_tokens.sum(axis=1).astype(jnp.bfloat16)]
  transfers between devices with their start and end apart: 4 -> 1, of which waited for: 3 -> 1; matrix products, arithmetic and copies ran while one was open for 17% -> 3% of each run, Pallas kernels for 0% -> 0%
where the time goes in v2:
time: 166 us
  Pallas kernels  80.2 us (48%)
  blocking collectives  45.8 us (28%)
  local copies, waits for them, and re-layouts  15.5 us (9%)
  waiting for transfers between devices  12 us (7%)
  starting transfers between devices  8.59 us (5%)
  other arithmetic  2.77 us (2%)
    pallas_call x1, Pallas kernels, body(): pl.pallas_call(functools.partial(expert_kernel, (n_dp, n_ex, slots, tok,...  80.2 us
    all_to_all x1, blocking collectives, body(): lax.all_to_all(a.reshape(n_ex, slots, -1), 'expert', split_axis=0, concat...  45.8 us
    all_to_all x1, waiting for transfers between devices, body(): lax.all_to_all(a.reshape(n_ex, slots, -1), 'expert', split_axis=0, concat...  12 us
    all_to_all x1, starting transfers between devices, body(): lax.all_to_all(a.reshape(n_ex, slots, -1), 'expert', split_axis=0, concat...  8.59 us
    scatter x1, local copies, waits for them, and re-layouts, body(): jnp.zeros((rows, width), BF16).at[position]  5.71 us
    unnamed x12, local copies, waits for them, and re-layouts  5.55 us
    scatter x1, local copies, waits for them, and re-layouts, body(): jnp.zeros((rows, hidden), BF16).at[position]  3.57 us
  transfers between devices with their start and end apart: 1, of which 1 were waited for; matrix products, arithmetic and copies ran while one was open for 3% of the time, Pallas kernels for 0%

profile of v2, /device:TPU:1, one launch (start us, length us, event | category | flops | bytes accessed | tf_op | source)
XLA Modules:
  0.0 165.5 jit_solution(6324027414159633218)
XLA Ops:
  0.6 0.0 copy-start
  0.6 0.8 copy.9
  1.5 0.1 eq.32
  1.6 0.1 eq.28
  1.7 0.1 reshape.258
  1.8 1.2 reduce-window.6
  3.0 0.2 slice_reduce_fusion
  3.3 0.1 fusion.21
  3.4 0.2 copy.17
  3.6 1.2 fusion.13
  4.8 0.1 fusion.14
  5.0 0.0 copy-done
  5.0 0.0 copy-start.3
  5.0 3.6 %scatter_custom_fusion.1 = bf16[768,768]{1,0:T(8,128)(2,1)} fusion(s32[512]{0:T(512)S(1)} %fusion.14, bf16[64,8,768]{2,1,0:T(8,128)(2,1)S(1)} %copy-done, bf16[]{:T(256)} %constant.48.clone.1), kind=kCustom, calls=%fused_computation.6 | custom fusion | bytes 1966082 | tf_op jit(solution)/shard_map/scatter | solution.py:228
  8.6 8.6 %all-to-all-start.1 = ((bf16[32,24,768]{2,1,0:T(8,128)(2,1)}), bf16[32,24,768]{2,1,0:T(8,128)(2,1)S(1)}, u32[]{:S(2)}, u32[]{:S(2)}) async-start(bf16[32,24,768]{2,1,0:T(8,128)(2,1)} %bitcast.6), calls=%async_computation.1 | async-start | bytes 2359296 | tf_op jit(solution)/shard_map/all_to_all | solution.py:230
  17.2 0.0 copy-done.3
  17.2 5.7 %scatter_custom_fusion = bf16[768,2048]{1,0:T(8,128)(2,1)} fusion(s32[512]{0:T(512)S(1)} %fusion.14, bf16[]{:T(256)} %constant.48.clone.1, bf16[64,2048]{1,0:T(8,128)(2,1)S(1)} %copy-done.3), kind=kCustom, calls=%fused_computation.2 | custom fusion | bytes 3407874 | tf_op jit(solution)/shard_map/scatter | solution.py:226
  22.9 12.0 %all-to-all-done.1 = bf16[32,24,768]{2,1,0:T(8,128)(2,1)S(1)} async-done(((bf16[32,24,768]{2,1,0:T(8,128)(2,1)}), bf16[32,24,768]{2,1,0:T(8,128)(2,1)S(1)}, u32[]{:S(2)}, u32[]{:S(2)}) %all-to-all-start.1) | async-done | bytes 1179680 | tf_op jit(solution)/shard_map/all_to_all | solution.py:230
  34.9 45.8 %all_to_all.10 = bf16[32,24,2048]{2,1,0:T(8,128)(2,1)} all-to-all(bf16[32,24,2048]{2,1,0:T(8,128)(2,1)} %bitcast.30), channel_id=1, replica_groups=mesh['dp'=8,'expert'=32] {'expert'}, dimensions={0} | all-to-all | bytes 6291456 | tf_op jit(solution)/shard_map/all_to_all | solution.py:230
  80.6 80.2 %expert_backward.1 = (bf16[64,2048]{1,0:T(8,128)(2,1)}, f32[256,768]{1,0:T(8,128)}, f32[256,768]{1,0:T(8,128)}) custom-call(bf16[768,2048]{1,0:T(8,128)(2,1)} %bitcast.31, bf16[768,768]{1,0:T(8,128)(2,1)} %bitcast.32, s32[512,1]{1,0:T(8,128)} %get-tuple-element.9.pos_ref, bf16[2048,768]{1,0:T(8,128)(2,1)} %bitcast.33, bf16[2048,768]{1,0:T(8,128)(2,1)} %bitcast.34), custom_call_target="tpu_custom_call" | custom-call | tf_op jit(solution)/shard_map/expert_backward/pallas_call | solution.py:240
  160.8 0.0 copy-start.2
  160.8 1.7 %copy.23 = bf16[64,2048]{1,0:T(8,128)(2,1)} copy(bf16[64,2048]{1,0:T(8,128)(2,1)} %get-tuple-element.14) | data formatting | bytes 524288
  162.6 2.1 %copy.24 = f32[1,256,768]{2,1,0:T(8,128)} copy(f32[1,256,768]{2,1,0:T(8,128)} %bitcast.36) | data formatting | bytes 1572864
  164.6 0.9 copy.25
  (6 shorter events, 0.1 us)
Async XLA Ops:
  0.6 4.4 %copy-start = (bf16[64,8,768]{2,1,0:T(8,128)(2,1)S(1)}, bf16[64,8,768]{2,1,0:T(8,128)(2,1)}, u32[]{:S(2)}) copy-start(bf16[64,8,768]{2,1,0:T(8,128)(2,1)} %param.6) | copy-start | bytes 2359300
  5.0 12.2 %copy-start.3 = (bf16[64,2048]{1,0:T(8,128)(2,1)S(1)}, bf16[64,2048]{1,0:T(8,128)(2,1)}, u32[]{:S(2)}) copy-start(bf16[64,2048]{1,0:T(8,128)(2,1)} %param.5) | copy-start | bytes 786436
  8.6 26.3 %all-to-all-start.1 = ((bf16[32,24,768]{2,1,0:T(8,128)(2,1)}), bf16[32,24,768]{2,1,0:T(8,128)(2,1)S(1)}, u32[]{:S(2)}, u32[]{:S(2)}) async-start(bf16[32,24,768]{2,1,0:T(8,128)(2,1)} %bitcast.6), calls=%async_computation.1 | async-start | bytes 2359296 | tf_op jit(solution)/shard_map/all_to_all | solution.py:230
  34.9 45.8 %copy-start.1 = (bf16[32,24,768]{2,1,0:T(8,128)(2,1)}, bf16[32,24,768]{2,1,0:T(8,128)(2,1)S(1)}, u32[]{:S(2)}) copy-start(bf16[32,24,768]{2,1,0:T(8,128)(2,1)S(1)} %all-to-all-done.1) | copy-start | bytes 3538948
  160.8 3.8 %copy-start.2 = (f32[256,768]{1,0:T(8,128)S(1)}, f32[256,768]{1,0:T(8,128)}, u32[]{:S(2)}) copy-start(f32[256,768]{1,0:T(8,128)} %get-tuple-element.8) | copy-start | bytes 2359300

commit v3 on v2

--- a/solution.py
+++ b/solution.py
@@ -9,37 +9,40 @@
 
 MESH = pl.DeviceIdType.MESH
 F32, BF16 = jnp.float32, jnp.bfloat16
-
-
-def slot_index(route_block, expert_count, capacity):
-    flat_routes = route_block.reshape(-1)
-    labels = jnp.arange(2 * expert_count, dtype=jnp.int32)
-    one_hot = (flat_routes[:, None] == labels[None, :]).astype(jnp.int32)
-    earlier = jnp.sum((jnp.cumsum(one_hot, axis=0) - 1) * one_hot, axis=1)
-    kind = flat_routes // expert_count
-    home = jnp.bitwise_xor(flat_routes % expert_count, kind * (expert_count // 2))
-    return (home * 2 + kind) * capacity + earlier
+SIDE = 4
 
 
 def expert_kernel(
     dims,
-    xs_ref, dh_ref, pos_ref, wg_hbm, wu_hbm,
+    row_ref, col_ref, x_hbm, cot_hbm, wg_hbm, wu_hbm,
     gt_ref, gg_ref, gu_ref,
     w_ref, d_ref, ring_ref, part_ref, back_ref, ret_ref, comb_ref,
+    cot_ref, xg_ref, xs_ref, dh_ref, dh_out, dh_in, all_ref, flat_ref, sel_ref,
     w_sem, ring_send, ring_recv, ret_send, ret_recv, own_sem,
+    in_sem, ag_send, ag_recv, sib_send, sib_recv, dh_send, dh_recv, r_send, r_recv,
 ):
     n_dp, n_ex, slots, tok, top = dims
     width, hidden = w_ref.shape[1], w_ref.shape[2]
-    rows = xs_ref.shape[0]
+    rows = n_ex * slots
     cols = width // n_dp
     half = cols // 2
     me = lax.axis_index("expert")
     p = lax.axis_index("dp")
+    core = lax.rem(me, 2)
+    mx, my = lax.rem(me // 2, SIDE), me // (2 * SIDE)
+    half_w = width // 2
+    own_rows = pl.ds(pl.multiple_of(core * tok, tok), tok)
+    loads = [
+        pltpu.make_async_copy(
+            x_hbm.at[:, pl.ds(h * half_w, half_w)], xg_ref.at[me // 2, h, own_rows], in_sem.at[h]
+        )
+        for h in range(2)
+    ] + [pltpu.make_async_copy(cot_hbm, cot_ref, in_sem.at[2])]
     w_copies = [
         pltpu.make_async_copy(src, w_ref.at[k], w_sem.at[k])
         for k, src in enumerate((wg_hbm, wu_hbm))
     ]
-    for c in w_copies:
+    for c in loads + w_copies:
         c.start()
     barrier = pltpu.get_barrier_semaphore()
     right, left = lax.rem(p + 1, n_dp), lax.rem(p + n_dp - 1, n_dp)
@@ -54,17 +57,233 @@
 
     lax.fori_loop(1, n_ex, greet, 0)
 
+    flat = tok * top
+    early = lax.broadcasted_iota(jnp.int32, (flat, flat), 0)
+    late = lax.broadcasted_iota(jnp.int32, (flat, flat), 1)
+    same = col_ref[...] == row_ref[...]
+    rank_row = jnp.sum(jnp.where(same & (early < late), 1.0, 0.0), axis=0, keepdims=True)
+    rank_col = jnp.sum(jnp.where(same & (late < early), 1.0, 0.0), axis=1, keepdims=True)
+
+    def placed(route, rank, stride):
+        kind = jnp.where(route >= n_ex, 1, 0)
+        home = route - kind * n_ex
+        home = jnp.where(kind == 1, jnp.where(home >= n_ex // 2, home - n_ex // 2, home + n_ex // 2), home)
+        return home * stride + kind * (slots // 2) + rank.astype(jnp.int32)
+
+    pos_row = placed(row_ref[...], rank_row, slots)
+    pos_col = placed(col_ref[...], rank_col, 2 * slots)
+
     wide = 2 * n_ex * slots
-    place = lax.broadcasted_iota(jnp.int32, (tok * top, wide), 1)
-    row_of = lax.broadcasted_iota(jnp.int32, (tok, tok * top), 1)
-    token_of = lax.broadcasted_iota(jnp.int32, (tok, tok * top), 0) * top
+    place = lax.broadcasted_iota(jnp.int32, (flat, wide), 1)
+    row_of = lax.broadcasted_iota(jnp.int32, (tok, flat), 1)
+    token_of = lax.broadcasted_iota(jnp.int32, (tok, flat), 0) * top
     group = jnp.where((row_of >= token_of) & (row_of < token_of + top), 1.0, 0.0).astype(BF16)
     for k in range(2):
-        hit = jnp.where(place == pos_ref[...] + k * slots, 1.0, 0.0).astype(BF16)
+        hit = jnp.where(place == pos_col + k * slots, 1.0, 0.0).astype(BF16)
         comb_ref[k * tok:(k + 1) * tok, :] = jnp.dot(
             group, hit, preferred_element_type=F32
         ).astype(BF16)
 
+    lot = 8
+    loads[2].wait()
+
+    def pack(i, c):
+        spot = lax.broadcasted_iota(jnp.int32, (lot * slots, flat), 0) + i * (lot * slots)
+        hit = jnp.where(spot == pos_row, 1.0, 0.0).astype(BF16)
+        v = jnp.dot(hit, cot_ref[...], preferred_element_type=F32).reshape(lot, slots, hidden)
+        for j in range(lot):
+            for k in range(2):
+                dh_out[i * lot + j, k * slots:(k + 1) * slots, :] = v[
+                    j, :, k * (hidden // 2):(k + 1) * (hidden // 2)
+                ].astype(BF16)
+        return c
+
+    lax.fori_loop(0, n_ex // lot, pack, 0)
+    all_ref[me] = row_ref[...]
+    for c in loads[:2]:
+        c.wait()
+
+    def chip_at(h, da, db):
+        dx, dy = (da, db) if h == 0 else (db, da)
+        return lax.rem(my + dy, SIDE) * SIDE + lax.rem(mx + dx, SIDE)
+
+    def off(da, db):
+        return (da % SIDE) * SIDE + db % SIDE
+
+    def slab(h, da, db, lo, n, of_core):
+        return xg_ref.at[
+            chip_at(h, da % SIDE, db % SIDE), h,
+            pl.ds(pl.multiple_of(of_core * tok + lo, tok // 2), n),
+        ]
+
+    sends = []
+
+    def pass_on(h, da, db, axis, sign, piece=None):
+        lo, n = (0, tok) if piece is None else (piece * (tok // 2), tok // 2)
+        ra, rb = (da - sign, db) if axis == 0 else (da, db - sign)
+        ta, tb = (sign % SIDE, 0) if axis == 0 else (0, sign % SIDE)
+        ref = slab(h, da, db, lo, n, core)
+        c = pltpu.make_async_remote_copy(
+            src_ref=ref, dst_ref=ref,
+            send_sem=ag_send.at[len(sends)],
+            recv_sem=ag_recv.at[h, off(ra, rb), piece or 0],
+            device_id={"expert": chip_at(h, ta, tb) * 2 + core},
+            device_id_type=MESH,
+        )
+        c.start()
+        sends.append(c)
+
+    def arrived(h, da, db, piece=None):
+        lo, n = (0, tok) if piece is None else (piece * (tok // 2), tok // 2)
+        ref = slab(h, da, db, lo, n, core)
+        pltpu.make_async_remote_copy(
+            src_ref=ref, dst_ref=ref, send_sem=ag_send.at[0],
+            recv_sem=ag_recv.at[h, off(da, db), piece or 0],
+            device_id={"expert": me}, device_id_type=MESH,
+        ).wait_recv()
+
+    def sibling(h, da, db, of_core):
+        ref = slab(h, da, db, 0, tok, of_core)
+        return pltpu.make_async_remote_copy(
+            src_ref=ref, dst_ref=ref,
+            send_sem=sib_send.at[h, off(da, db)],
+            recv_sem=sib_recv.at[h, off(da, db)],
+            device_id={"expert": me + 1 - 2 * core},
+            device_id_type=MESH,
+        )
+
+    def share(h, da, db):
+        sibling(h, da, db, core).start()
+
+    def select(h, da, db):
+        sibling(h, da, db, 1 - core).wait_recv()
+        chip = chip_at(h, da % SIDE, db % SIDE)
+        xs_ref[
+            pl.ds(pl.multiple_of(chip * 2 * slots, 2 * slots), 2 * slots),
+            h * half_w:(h + 1) * half_w,
+        ] = jnp.dot(sel_ref[chip], xg_ref[chip, h], preferred_element_type=F32).astype(BF16)
+
+    def route_copy(t, slot):
+        return pltpu.make_async_remote_copy(
+            src_ref=all_ref.at[me], dst_ref=all_ref.at[slot],
+            send_sem=r_send.at[t], recv_sem=r_recv.at[slot],
+            device_id={"expert": t}, device_id_type=MESH,
+        )
+
+    def dh_copy(t, slot):
+        return pltpu.make_async_remote_copy(
+            src_ref=dh_out.at[t], dst_ref=dh_in.at[slot],
+            send_sem=dh_send.at[t], recv_sem=dh_recv.at[slot],
+            device_id={"expert": t}, device_id_type=MESH,
+        )
+
+    def peers(go):
+        def one(k, c):
+            go(lax.rem(me + k, n_ex))
+            return c
+
+        lax.fori_loop(1, n_ex, one, 0)
+
+    pl.semaphore_wait(barrier, n_ex + 1)
+    peers(lambda t: route_copy(t, me).start())
+    for h in range(2):
+        for sign in (1, -1):
+            pass_on(h, 0, 0, 0, sign)
+    for h in range(2):
+        for sign in (1, -1):
+            pass_on(h, 0, 0, 1, sign)
+        share(h, 0, 0)
+
+    peers(lambda t: route_copy(t, t).wait())
+    for s in range(n_ex):
+        flat_ref[s:s + 1, :] = all_ref[s].astype(F32)
+    named = flat_ref[...]
+    here = me.astype(F32)
+    other = jnp.where(me >= n_ex // 2, me - n_ex // 2, me + n_ex // 2) + n_ex
+    kinds = [jnp.where(named == v, 1.0, 0.0) for v in (here, other.astype(F32))]
+    prior = jnp.where(early < late, 1.0, 0.0).astype(BF16)
+    ranks = jnp.dot(
+        jnp.concatenate(kinds, axis=0).astype(BF16), prior, preferred_element_type=F32
+    )
+    flat_ref[...] = (
+        kinds[0] * (ranks[:n_ex] + 1.0) + kinds[1] * (ranks[n_ex:] + (1.0 + slots // 2)) - 1.0
+    )
+    token_lane = lax.broadcasted_iota(jnp.int32, (flat, 2 * tok), 1)
+    token_lane = jnp.where(token_lane >= tok, token_lane - tok, token_lane) * top
+    from_row = lax.broadcasted_iota(jnp.int32, (flat, 2 * tok), 0)
+    to_token = jnp.where(
+        (from_row >= token_lane) & (from_row < token_lane + top), 1.0, 0.0
+    ).astype(BF16)
+    spot_row = lax.broadcasted_iota(jnp.int32, (2 * slots, 2 * tok), 0) >= slots
+    spot_lane = lax.broadcasted_iota(jnp.int32, (2 * slots, 2 * tok), 1) >= tok
+    slot_no = lax.broadcasted_iota(jnp.int32, (slots, flat), 0).astype(F32)
+
+    def choose(i, c):
+        hits = [
+            jnp.where(slot_no == flat_ref[pl.ds(2 * i + k, 1), :], 1.0, 0.0) for k in range(2)
+        ]
+        v = jnp.dot(
+            jnp.concatenate(hits, axis=0).astype(BF16), to_token, preferred_element_type=F32
+        )
+        sel_ref[i] = jnp.where(spot_row == spot_lane, v, 0.0).astype(BF16)
+        return c
+
+    lax.fori_loop(0, n_ex // 2, choose, 0)
+
+    both_ways = [(h, sign) for h in range(2) for sign in (1, -1)]
+    for h, sign in both_ways:
+        arrived(h, -sign, 0)
+        pass_on(h, -sign, 0, 0, sign, 0 if sign == 1 else 1)
+        pass_on(h, -sign, 0, 1, 1)
+        pass_on(h, -sign, 0, 1, -1)
+        share(h, -sign, 0)
+    for h, sign in both_ways:
+        arrived(h, 0, -sign)
+        pass_on(h, 0, -sign, 1, sign, 0 if sign == 1 else 1)
+        share(h, 0, -sign)
+    for h in range(2):
+        select(h, 0, 0)
+    for h in range(2):
+        for piece in range(2):
+            arrived(h, 2, 0, piece)
+        for sign in (1, -1):
+            pass_on(h, 2, 0, 1, sign)
+        share(h, 2, 0)
+    for h in range(2):
+        for da in (1, -1):
+            select(h, da, 0)
+    for da in (1, -1, 2):
+        for h, sign in both_ways:
+            arrived(h, da, -sign)
+            pass_on(h, da, -sign, 1, sign, 0 if sign == 1 else 1)
+            share(h, da, -sign)
+    peers(lambda t: dh_copy(t, me).start())
+    dh_own = pltpu.make_async_copy(dh_out.at[me], dh_in.at[me], in_sem.at[3])
+    dh_own.start()
+    for h in range(2):
+        for da, db in ((0, 1), (0, -1), (2, 0), (1, 1), (1, -1), (-1, 1), (-1, -1)):
+            select(h, da, db)
+    for da in (0, 1, -1, 2):
+        for h in range(2):
+            for piece in range(2):
+                arrived(h, da, 2, piece)
+            share(h, da, 2)
+    for h in range(2):
+        for da, db in ((2, 1), (2, -1), (0, 2), (1, 2), (-1, 2), (2, 2)):
+            select(h, da, db)
+    peers(lambda t: dh_copy(t, t).wait())
+    dh_own.wait()
+
+    def unpack(i, c):
+        v = dh_in[pl.ds(2 * i, 2)].astype(F32)
+        r = pl.ds(pl.multiple_of(i * 2 * slots, 2 * slots), 2 * slots)
+        for k in range(2):
+            dh_ref[r, k * (hidden // 2):(k + 1) * (hidden // 2)] = (
+                v[:, k * slots:(k + 1) * slots].reshape(2 * slots, hidden // 2).astype(BF16)
+            )
+        return c
+
+    lax.fori_loop(0, n_ex // 2, unpack, 0)
     for c in w_copies:
         c.wait()
     m_blk, n_blk = rows // 2, 256
@@ -104,7 +323,6 @@
             device_id_type=MESH,
         )
 
-    pl.semaphore_wait(barrier, n_ex + 1)
     for k in range(2):
         ring_ref[k, 0] = part(chunk(0, k), k).astype(BF16)
         for b in range(2):
@@ -211,6 +429,12 @@
         return c
 
     lax.fori_loop(0, n_dp - 1, sent, 0)
+    for c in sends:
+        c.wait_send()
+    for h in range(2):
+        for da in range(SIDE):
+            for db in range(SIDE):
+                sibling(h, da, db, core).wait_send()
 
 
 def body(tokens, row_cotangent, routes, w_gate, w_up):
@@ -221,18 +445,7 @@
     capacity = 3 * tok * top // (4 * n_ex)
     slots = 2 * capacity
     rows = n_ex * slots
-    position = slot_index(routes, n_ex, capacity)
-    send_x = (
-        jnp.zeros((rows, width), BF16).at[position].set(jnp.repeat(tokens, top, axis=0))
-    )
-    send_d = jnp.zeros((rows, hidden), BF16).at[position].set(row_cotangent.reshape(-1, hidden))
-    recv_x, recv_d = (
-        lax.all_to_all(
-            a.reshape(n_ex, slots, -1), "expert", split_axis=0, concat_axis=0, tiled=True
-        ).reshape(rows, -1)
-        for a in (send_x, send_d)
-    )
-    pos_col = (position // slots * (2 * slots) + position % slots)[:, None]
+    flat = tok * top
     vmem = pl.BlockSpec(memory_space=pltpu.VMEM)
     hbm = pl.BlockSpec(memory_space=pl.ANY)
     cols = width // n_dp
@@ -244,7 +457,7 @@
             jax.ShapeDtypeStruct((cols, hidden), F32),
             jax.ShapeDtypeStruct((cols, hidden), F32),
         ),
-        in_specs=[vmem, vmem, vmem, hbm, hbm],
+        in_specs=[vmem, vmem, hbm, hbm, hbm, hbm],
         out_specs=(vmem, vmem, vmem),
         scratch_shapes=[
             pltpu.VMEM((2, width, hidden), BF16),
@@ -254,18 +467,39 @@
             pltpu.VMEM((n_ex, 2 * slots, width // 2), BF16),
             pltpu.VMEM((n_ex, 2 * slots, width // 2), BF16),
             pltpu.VMEM((2 * tok, 2 * rows), BF16),
+            pltpu.VMEM((flat, hidden), BF16),
+            pltpu.VMEM((n_ex // 2, 2, 2 * tok, width // 2), BF16),
+            pltpu.VMEM((rows, width), BF16),
+            pltpu.VMEM((rows, hidden), BF16),
+            pltpu.VMEM((n_ex, 2 * slots, hidden // 2), BF16),
+            pltpu.VMEM((n_ex, 2 * slots, hidden // 2), BF16),
+            pltpu.VMEM((n_ex, 1, flat), jnp.int32),
+            pltpu.VMEM((n_ex, flat), F32),
+            pltpu.VMEM((n_ex // 2, 2 * slots, 2 * tok), BF16),
             dma((2,)),
             dma((2, n_dp, 2)),
             dma((2, n_dp, 2)),
             dma((n_ex,)),
             dma((n_ex,)),
             dma,
+            dma((4,)),
+            dma((40,)),
+            dma((2, SIDE * SIDE, 2)),
+            dma((2, SIDE * SIDE)),
+            dma((2, SIDE * SIDE)),
+            dma((n_ex,)),
+            dma((n_ex,)),
+            dma((n_ex,)),
+            dma((n_ex,)),
         ],
         compiler_params=pltpu.CompilerParams(
             collective_id=0, has_side_effects=True, vmem_limit_bytes=56 << 20
         ),
         name="expert_backward",
-    )(recv_x, recv_d, pos_col, w_gate[0], w_up[0])
+    )(
+        routes.reshape(1, flat), routes.reshape(flat, 1), tokens,
+        row_cotangent.reshape(flat, hidden), w_gate[0], w_up[0],
+    )
     return gt, gg[None], gu[None]
 
 

time: 166 us -> 134 us (0.81)
  blocking collectives: 45.8 us -> 0 us
  Pallas kernels: 80.2 us -> 125 us
  waiting for transfers between devices: 12 us -> 0 us
  starting transfers between devices: 8.59 us -> 0 us
  local copies, waits for them, and re-layouts: 15.5 us -> 8.07 us
  other arithmetic: 2.77 us -> 0 us
    all_to_all x1 -> x0, blocking collectives: 45.8 us -> none  [body(): lax.all_to_all(a.reshape(n_ex, slots, -1), 'expert', split_axis=0, concat...]
    pallas_call x1, Pallas kernels: 80.2 us -> 125 us  [body(): pl.pallas_call(functools.partial(expert_kernel, (n_dp, n_ex, slots, tok,...]
    all_to_all x1 -> x0, waiting for transfers between devices: 12 us -> none  [body(): lax.all_to_all(a.reshape(n_ex, slots, -1), 'expert', split_axis=0, concat...]
    scatter x2 -> x0, local copies, waits for them, and re-layouts: 9.29 us -> none  [the longest x1 5.71 us: body(): jnp.zeros((rows, width), BF16).at[position]]
    all_to_all x1 -> x0, starting transfers between devices: 8.59 us -> none  [body(): lax.all_to_all(a.reshape(n_ex, slots, -1), 'expert', split_axis=0, concat...]
    unnamed x12 -> x4, local copies, waits for them, and re-layouts: 5.55 us -> 6.57 us
  transfers between devices with their start and end apart: 1 -> 0, of which waited for: 1 -> 0; matrix products, arithmetic and copies ran while one was open for 3% -> 0% of each run, Pallas kernels for 0% -> 0%
where the time goes in v3:
time: 134 us
  Pallas kernels  125 us (93%)
  local copies, waits for them, and re-layouts  8.07 us (6%)
    pallas_call x1, Pallas kernels, body(): pl.pallas_call(functools.partial(expert_kernel, (n_dp, n_ex, slots, tok,...  125 us
    unnamed x4, local copies, waits for them, and re-layouts  6.57 us

profile of v3, /device:TPU:1, one launch (start us, length us, event | category | flops | bytes accessed | tf_op | source)
XLA Modules:
  0.0 134.2 jit_solution(7568311432303144064)
XLA Ops:
  0.6 0.8 copy.10
  1.4 0.7 reshape.15.row_ref
  2.1 0.8 reshape.18.col_ref
  2.9 125.4 %expert_backward.1 = (bf16[64,2048]{1,0:T(8,128)(2,1)}, f32[256,768]{1,0:T(8,128)}, f32[256,768]{1,0:T(8,128)}) custom-call(s32[1,512]{1,0:T(1,128)} %reshape.15.row_ref, s32[512,1]{1,0:T(8,128)} %reshape.18.col_ref, bf16[64,2048]{1,0:T(8,128)(2,1)} %x_hbm.1, bf16[512,768]{1,0:T(8,128)(2,1)} %bitcast.7, bf16[2048,768]{1,0:T(8,128)(2,1)} %bitcast.5, ...), custom_call_target="tpu_custom_call" | custom-call | tf_op jit(solution)/shard_map/expert_backward/pallas_call | solution.py:453
  128.4 1.7 %copy.16 = bf16[64,2048]{1,0:T(8,128)(2,1)} copy(bf16[64,2048]{1,0:T(8,128)(2,1)} %get-tuple-element.12) | data formatting | bytes 524288
  130.0 2.1 %copy.17 = f32[1,256,768]{2,1,0:T(8,128)} copy(f32[1,256,768]{2,1,0:T(8,128)} %bitcast.9) | data formatting | bytes 1572864
  132.1 2.1 %copy.18 = f32[1,256,768]{2,1,0:T(8,128)} copy(f32[1,256,768]{2,1,0:T(8,128)} %bitcast.8) | data formatting | bytes 1572864

commit v4 on v3

--- a/solution.py
+++ b/solution.py
@@ -10,14 +10,18 @@
 MESH = pl.DeviceIdType.MESH
 F32, BF16 = jnp.float32, jnp.bfloat16
 SIDE = 4
+ROUND = (
+    (1, 0), (3, 0), (0, 1), (0, 3), (1, 1), (3, 3), (1, 3), (3, 1),
+    (2, 0), (0, 2), (2, 1), (1, 2), (2, 3), (3, 2), (2, 2),
+)
 
 
 def expert_kernel(
     dims,
-    row_ref, col_ref, x_hbm, cot_hbm, wg_hbm, wu_hbm,
+    routes_ref, x_hbm, cot_hbm, wg_hbm, wu_hbm,
     gt_ref, gg_ref, gu_ref,
     w_ref, d_ref, ring_ref, part_ref, back_ref, ret_ref, comb_ref,
-    cot_ref, xg_ref, xs_ref, dh_ref, dh_out, dh_in, all_ref, flat_ref, sel_ref,
+    cot_ref, xg_ref, xs_ref, gate_ref, dh_out, dh_in, all_ref, flat_ref, sel_ref,
     w_sem, ring_send, ring_recv, ret_send, ret_recv, own_sem,
     in_sem, ag_send, ag_recv, sib_send, sib_recv, dh_send, dh_recv, r_send, r_recv,
 ):
@@ -25,7 +29,8 @@
     width, hidden = w_ref.shape[1], w_ref.shape[2]
     rows = n_ex * slots
     cols = width // n_dp
-    half = cols // 2
+    third = hidden // 3
+    lane = third // 2
     me = lax.axis_index("expert")
     p = lax.axis_index("dp")
     core = lax.rem(me, 2)
@@ -60,24 +65,35 @@
     flat = tok * top
     early = lax.broadcasted_iota(jnp.int32, (flat, flat), 0)
     late = lax.broadcasted_iota(jnp.int32, (flat, flat), 1)
-    same = col_ref[...] == row_ref[...]
-    rank_row = jnp.sum(jnp.where(same & (early < late), 1.0, 0.0), axis=0, keepdims=True)
-    rank_col = jnp.sum(jnp.where(same & (late < early), 1.0, 0.0), axis=1, keepdims=True)
-
-    def placed(route, rank, stride):
-        kind = jnp.where(route >= n_ex, 1, 0)
-        home = route - kind * n_ex
-        home = jnp.where(kind == 1, jnp.where(home >= n_ex // 2, home - n_ex // 2, home + n_ex // 2), home)
-        return home * stride + kind * (slots // 2) + rank.astype(jnp.int32)
-
-    pos_row = placed(row_ref[...], rank_row, slots)
-    pos_col = placed(col_ref[...], rank_col, 2 * slots)
-
-    wide = 2 * n_ex * slots
-    place = lax.broadcasted_iota(jnp.int32, (flat, wide), 1)
     row_of = lax.broadcasted_iota(jnp.int32, (tok, flat), 1)
     token_of = lax.broadcasted_iota(jnp.int32, (tok, flat), 0) * top
     group = jnp.where((row_of >= token_of) & (row_of < token_of + top), 1.0, 0.0).astype(BF16)
+    named = routes_ref[...].astype(F32).astype(BF16)
+    over_first = (((0,), (0,)), ((), ()))
+    by_row = jnp.dot(named, group, preferred_element_type=F32)
+    by_col = lax.dot_general(group, named, (((0,), (1,)), ((), ())), preferred_element_type=F32)
+    j_row = lax.broadcasted_iota(jnp.int32, (top, flat), 0)
+    j_col = lax.broadcasted_iota(jnp.int32, (flat, top), 1)
+    at_row = lax.rem(lax.broadcasted_iota(jnp.int32, (top, flat), 1), top)
+    at_col = lax.rem(lax.broadcasted_iota(jnp.int32, (flat, top), 0), top)
+    route_row = jnp.sum(jnp.where(j_row == at_row, by_row, 0.0), axis=0, keepdims=True)
+    route_col = jnp.sum(jnp.where(j_col == at_col, by_col, 0.0), axis=1, keepdims=True)
+    same = route_col == route_row
+    rank_row = jnp.sum(jnp.where(same & (early < late), 1.0, 0.0), axis=0, keepdims=True)
+    rank_col = jnp.sum(jnp.where(same & (late < early), 1.0, 0.0), axis=1, keepdims=True)
+
+    def placed(route, rank, stride):
+        kind = jnp.where(route >= n_ex, 1.0, 0.0)
+        home = route - kind * n_ex
+        away = jnp.where(home >= n_ex // 2, home - n_ex // 2, home + n_ex // 2)
+        home = jnp.where(kind > 0.5, away, home)
+        return (home * stride + kind * (slots // 2) + rank).astype(jnp.int32)
+
+    pos_row = placed(route_row, rank_row, slots)
+    pos_col = placed(route_col, rank_col, 2 * slots)
+
+    wide = 2 * n_ex * slots
+    place = lax.broadcasted_iota(jnp.int32, (flat, wide), 1)
     for k in range(2):
         hit = jnp.where(place == pos_col + k * slots, 1.0, 0.0).astype(BF16)
         comb_ref[k * tok:(k + 1) * tok, :] = jnp.dot(
@@ -92,14 +108,14 @@
         hit = jnp.where(spot == pos_row, 1.0, 0.0).astype(BF16)
         v = jnp.dot(hit, cot_ref[...], preferred_element_type=F32).reshape(lot, slots, hidden)
         for j in range(lot):
-            for k in range(2):
+            for k in range(6):
                 dh_out[i * lot + j, k * slots:(k + 1) * slots, :] = v[
-                    j, :, k * (hidden // 2):(k + 1) * (hidden // 2)
+                    j, :, k * lane:(k + 1) * lane
                 ].astype(BF16)
         return c
 
     lax.fori_loop(0, n_ex // lot, pack, 0)
-    all_ref[me] = row_ref[...]
+    all_ref[me] = route_row
     for c in loads[:2]:
         c.wait()
 
@@ -170,10 +186,13 @@
             device_id={"expert": t}, device_id_type=MESH,
         )
 
-    def dh_copy(t, slot):
+    def dh_piece(ref, q):
+        return ref.at[pl.ds(q * 2 * slots, 2 * (q + 1) * slots)]
+
+    def dh_copy(t, slot, q):
         return pltpu.make_async_remote_copy(
-            src_ref=dh_out.at[t], dst_ref=dh_in.at[slot],
-            send_sem=dh_send.at[t], recv_sem=dh_recv.at[slot],
+            src_ref=dh_piece(dh_out.at[t], q), dst_ref=dh_piece(dh_in.at[slot], q),
+            send_sem=dh_send.at[q, t], recv_sem=dh_recv.at[q, slot],
             device_id={"expert": t}, device_id_type=MESH,
         )
 
@@ -184,19 +203,45 @@
 
         lax.fori_loop(1, n_ex, one, 0)
 
+    def to_peers(go):
+        for dx, dy in ROUND:
+            for dc in range(2):
+                go(chip_at(0, dx, dy) * 2 + lax.rem(core + dc, 2))
+        go(me + 1 - 2 * core)
+
     pl.semaphore_wait(barrier, n_ex + 1)
-    peers(lambda t: route_copy(t, me).start())
     for h in range(2):
         for sign in (1, -1):
             pass_on(h, 0, 0, 0, sign)
+    peers(lambda t: route_copy(t, me).start())
     for h in range(2):
         for sign in (1, -1):
             pass_on(h, 0, 0, 1, sign)
         share(h, 0, 0)
+    to_peers(lambda t: dh_copy(t, me, 0).start())
+
+    both_ways = [(h, sign) for h in range(2) for sign in (1, -1)]
+    for h, sign in both_ways:
+        arrived(h, -sign, 0)
+        pass_on(h, -sign, 0, 0, sign, 0 if sign == 1 else 1)
+    for h, sign in both_ways:
+        pass_on(h, -sign, 0, 1, 1)
+        pass_on(h, -sign, 0, 1, -1)
+        share(h, -sign, 0)
+    for h, sign in both_ways:
+        arrived(h, 0, -sign)
+        pass_on(h, 0, -sign, 1, sign, 0 if sign == 1 else 1)
+        share(h, 0, -sign)
+    for h in range(2):
+        for piece in range(2):
+            arrived(h, 2, 0, piece)
+        for sign in (1, -1):
+            pass_on(h, 2, 0, 1, sign)
+        share(h, 2, 0)
 
     peers(lambda t: route_copy(t, t).wait())
     for s in range(n_ex):
-        flat_ref[s:s + 1, :] = all_ref[s].astype(F32)
+        flat_ref[s:s + 1, :] = all_ref[s]
     named = flat_ref[...]
     here = me.astype(F32)
     other = jnp.where(me >= n_ex // 2, me - n_ex // 2, me + n_ex // 2) + n_ex
@@ -230,25 +275,8 @@
 
     lax.fori_loop(0, n_ex // 2, choose, 0)
 
-    both_ways = [(h, sign) for h in range(2) for sign in (1, -1)]
-    for h, sign in both_ways:
-        arrived(h, -sign, 0)
-        pass_on(h, -sign, 0, 0, sign, 0 if sign == 1 else 1)
-        pass_on(h, -sign, 0, 1, 1)
-        pass_on(h, -sign, 0, 1, -1)
-        share(h, -sign, 0)
-    for h, sign in both_ways:
-        arrived(h, 0, -sign)
-        pass_on(h, 0, -sign, 1, sign, 0 if sign == 1 else 1)
-        share(h, 0, -sign)
     for h in range(2):
         select(h, 0, 0)
-    for h in range(2):
-        for piece in range(2):
-            arrived(h, 2, 0, piece)
-        for sign in (1, -1):
-            pass_on(h, 2, 0, 1, sign)
-        share(h, 2, 0)
     for h in range(2):
         for da in (1, -1):
             select(h, da, 0)
@@ -257,7 +285,6 @@
             arrived(h, da, -sign)
             pass_on(h, da, -sign, 1, sign, 0 if sign == 1 else 1)
             share(h, da, -sign)
-    peers(lambda t: dh_copy(t, me).start())
     dh_own = pltpu.make_async_copy(dh_out.at[me], dh_in.at[me], in_sem.at[3])
     dh_own.start()
     for h in range(2):
@@ -268,83 +295,105 @@
             for piece in range(2):
                 arrived(h, da, 2, piece)
             share(h, da, 2)
+    to_peers(lambda t: dh_copy(t, me, 1).start())
     for h in range(2):
         for da, db in ((2, 1), (2, -1), (0, 2), (1, 2), (-1, 2), (2, 2)):
             select(h, da, db)
-    peers(lambda t: dh_copy(t, t).wait())
-    dh_own.wait()
-
-    def unpack(i, c):
-        v = dh_in[pl.ds(2 * i, 2)].astype(F32)
-        r = pl.ds(pl.multiple_of(i * 2 * slots, 2 * slots), 2 * slots)
-        for k in range(2):
-            dh_ref[r, k * (hidden // 2):(k + 1) * (hidden // 2)] = (
-                v[:, k * slots:(k + 1) * slots].reshape(2 * slots, hidden // 2).astype(BF16)
-            )
-        return c
-
-    lax.fori_loop(0, n_ex // 2, unpack, 0)
     for c in w_copies:
         c.wait()
-    m_blk, n_blk = rows // 2, 256
-
-    def gates(i, c):
-        r = pl.ds(pl.multiple_of(i * m_blk, m_blk), m_blk)
-        for n in range(hidden // n_blk):
-            cs = slice(n * n_blk, (n + 1) * n_blk)
-            g = jnp.dot(xs_ref[r, :], w_ref[0, :, cs], preferred_element_type=F32)
-            u = jnp.dot(xs_ref[r, :], w_ref[1, :, cs], preferred_element_type=F32)
-            s = jax.nn.sigmoid(g)
-            h = dh_ref[r, cs].astype(F32)
-            d_ref[r, cs] = (h * u * s * (1.0 + g * (1.0 - s))).astype(BF16)
-            d_ref[r, hidden + n * n_blk:hidden + (n + 1) * n_blk] = (h * g * s).astype(BF16)
-        return c
-
-    lax.fori_loop(0, 2, gates, 0)
-
-    def part(c, k):
+    m_blk = rows // 2
+
+    def gates(b):
+        def one(i, c):
+            r = pl.ds(pl.multiple_of(i * m_blk, m_blk), m_blk)
+            for k in range(2):
+                gate_ref[k, r] = jnp.dot(
+                    xs_ref[r, :], w_ref[k, :, b * third:(b + 1) * third],
+                    preferred_element_type=F32,
+                )
+            return c
+
+        lax.fori_loop(0, 2, one, 0)
+
+    def cotangents(b):
+        def one(i, c):
+            n = 2 * slots
+            r = pl.ds(pl.multiple_of(i * n, n), n)
+            v = dh_in[pl.ds(2 * i, 2), b * n:(b + 1) * n].astype(F32)
+            for k in range(2):
+                cs = slice(k * lane, (k + 1) * lane)
+                h = v[:, k * slots:(k + 1) * slots].reshape(n, lane)
+                g, u = gate_ref[0, r, cs], gate_ref[1, r, cs]
+                s = jax.nn.sigmoid(g)
+                at = b * third + k * lane
+                d_ref[r, at:at + lane] = (h * u * s * (1.0 + g * (1.0 - s))).astype(BF16)
+                d_ref[r, hidden + at:hidden + at + lane] = (h * g * s).astype(BF16)
+            return c
+
+        lax.fori_loop(0, n_ex // 2, one, 0)
+
+    def part(c, k, b):
         x_cols = xs_ref[:, pl.ds(pl.multiple_of(c * cols, cols), cols)]
+        at = k * hidden + b * third
         return lax.dot_general(
-            x_cols, d_ref[:, k * hidden:(k + 1) * hidden],
-            (((0,), (0,)), ((), ())), preferred_element_type=F32,
+            x_cols, d_ref[:, at:at + third], over_first, preferred_element_type=F32
         )
 
     def chunk(s, k):
-        return lax.rem(p + n_dp - 1 - s, n_dp) if k == 0 else lax.rem(p + 1 + s, n_dp)
+        return lax.rem(p + 2 * n_dp - 1 - s, n_dp) if k == 0 else lax.rem(p + 1 + s, n_dp)
 
     def ring_copy(s, k, b):
-        sl = pl.ds(b * half, half)
         return pltpu.make_async_remote_copy(
-            src_ref=ring_ref.at[k, s, sl],
-            dst_ref=ring_ref.at[k, s + 1, sl],
+            src_ref=ring_ref.at[k, s, b],
+            dst_ref=ring_ref.at[k, s + 1, b],
             send_sem=ring_send.at[k, s, b],
             recv_sem=ring_recv.at[k, s, b],
             device_id={"dp": right if k == 0 else left},
             device_id_type=MESH,
         )
 
-    for k in range(2):
-        ring_ref[k, 0] = part(chunk(0, k), k).astype(BF16)
-        for b in range(2):
+    def begin(b):
+        gates(b)
+        if b == 0:
+            peers(lambda t: dh_copy(t, t, 0).wait())
+            dh_own.wait()
+        if b == 1:
+            peers(lambda t: dh_copy(t, t, 1).wait())
+        cotangents(b)
+        for k in range(2):
+            ring_ref[k, 0, b] = part(chunk(0, k), k, b).astype(BF16)
             ring_copy(0, k, b).start()
-
+        for k in range(2):
+            part_ref[k, b] = part(chunk(1, k), k, b)
+
+    def unit(s, b):
+        for k in range(2):
+            ring_copy(s - 1, k, b).wait_recv()
+            ring_ref[k, s, b] = (ring_ref[k, s, b].astype(F32) + part_ref[k, b]).astype(BF16)
+            ring_copy(s, k, b).start()
+        for k in range(2):
+            part_ref[k, b] = part(chunk(s + 1, k), k, b)
+
+    begin(0)
+    begin(1)
+    unit(1, 0)
+    begin(2)
     side = 8
     wide_col = width // 2
 
-    def back_chunk(i):
+    def back_half(i, h):
         y = lax.rem(me // side + i, n_ex // side)
         r = pl.ds(pl.multiple_of(y * side * slots, side * slots), side * slots)
-        for h in range(2):
-            wc = slice(h * wide_col, (h + 1) * wide_col)
-            dims_back = (((1,), (1,)), ((), ()))
-            b = lax.dot_general(
-                d_ref[r, :hidden], w_ref[0, wc, :], dims_back, preferred_element_type=F32
-            ) + lax.dot_general(
-                d_ref[r, hidden:], w_ref[1, wc, :], dims_back, preferred_element_type=F32
-            )
-            part_rows = b.reshape(side, slots, wide_col)
-            for j in range(side):
-                back_ref[y * side + j, h * slots:(h + 1) * slots, :] = part_rows[j].astype(BF16)
+        wc = slice(h * wide_col, (h + 1) * wide_col)
+        dims_back = (((1,), (1,)), ((), ()))
+        b = lax.dot_general(
+            d_ref[r, :hidden], w_ref[0, wc, :], dims_back, preferred_element_type=F32
+        ) + lax.dot_general(
+            d_ref[r, hidden:], w_ref[1, wc, :], dims_back, preferred_element_type=F32
+        )
+        part_rows = b.reshape(side, slots, wide_col)
+        for j in range(side):
+            back_ref[y * side + j, h * slots:(h + 1) * slots, :] = part_rows[j].astype(BF16)
         return y
 
     def ret_copy(t):
@@ -360,52 +409,36 @@
     own_copy = pltpu.make_async_copy(back_ref.at[me], ret_ref.at[me], own_sem)
 
     def start_returns(i, y):
-        def go(j, c):
-            ret_copy(y * side + lax.rem(me + j, side)).start()
-            return c
-
         if i == 0:
             own_copy.start()
-            lax.fori_loop(1, side, go, 0)
-        else:
-            lax.fori_loop(0, side, go, 0)
-
-    def ring_step(s):
-        for k in range(2):
-            part_ref[k] = part(chunk(s, k), k)
-        for b in range(2):
-            sl = pl.ds(b * half, half)
-            for k in range(2):
-                ring_copy(s - 1, k, b).wait_recv()
-                ring_ref[k, s, sl] = (
-                    ring_ref[k, s, sl].astype(F32) + part_ref[k, sl]
-                ).astype(BF16)
-                ring_copy(s, k, b).start()
-
-    start_returns(0, back_chunk(0))
-    ring_step(1)
-
-    def both(s, c):
-        start_returns(1, back_chunk(s - 1))
-        ring_step(s)
+        for dx in (1, 3, 0, 2):
+            for dc in range(2):
+                if (i, dx, dc) != (0, 0, 0):
+                    ret_copy(y * side + lax.rem(mx + dx, SIDE) * 2 + lax.rem(core + dc, 2)).start()
+
+    back_half(0, 0)
+    unit(1, 1)
+    start_returns(0, back_half(0, 1))
+    unit(1, 2)
+    back_half(1, 0)
+    unit(2, 0)
+    start_returns(1, back_half(1, 1))
+    unit(2, 1)
+    back_half(3, 0)
+    unit(2, 2)
+    start_returns(3, back_half(3, 1))
+    unit(3, 0)
+    back_half(2, 0)
+    unit(3, 1)
+    start_returns(2, back_half(2, 1))
+    unit(3, 2)
+
+    def alone(s, c):
+        for b in range(3):
+            unit(s, b)
         return c
 
-    lax.fori_loop(2, 5, both, 0)
-
-    def alone(s, c):
-        ring_step(s)
-        return c
-
-    lax.fori_loop(5, n_dp - 1, alone, 0)
-    scale = 1.0 / n_dp
-    for k in range(2):
-        part_ref[k] = part(p, k)
-    for b in range(2):
-        sl = pl.ds(b * half, half)
-        for k, out in enumerate((gg_ref, gu_ref)):
-            ring_copy(n_dp - 2, k, b).wait_recv()
-            out[sl] = (ring_ref[k, n_dp - 1, sl].astype(F32) + part_ref[k, sl]) * scale
-
+    lax.fori_loop(4, n_dp - 1, alone, 0)
     def got(j, c):
         t = lax.rem(me + j, n_ex)
         pltpu.make_async_remote_copy(
@@ -422,9 +455,17 @@
     gt_ref[:, :wide_col] = summed[:tok].astype(BF16)
     gt_ref[:, wide_col:] = summed[tok:].astype(BF16)
 
+    scale = 1.0 / n_dp
+    for b in range(3):
+        for k, out in enumerate((gg_ref, gu_ref)):
+            ring_copy(n_dp - 2, k, b).wait_recv()
+            out[:, b * third:(b + 1) * third] = (
+                ring_ref[k, n_dp - 1, b].astype(F32) + part_ref[k, b]
+            ) * scale
+
     def sent(s, c):
         for k in range(2):
-            for b in range(2):
+            for b in range(3):
                 ring_copy(s, k, b).wait_send()
         return c
 
@@ -435,6 +476,24 @@
         for da in range(SIDE):
             for db in range(SIDE):
                 sibling(h, da, db, core).wait_send()
+
+
+def hand_over(a, b, c, x, y, z, u, v, w, sem):
+    loads = [
+        pltpu.make_async_copy(src, held, sem.at[0, k])
+        for k, (src, held) in enumerate(((a, u), (b, v), (c, w)))
+    ]
+    stores = [
+        pltpu.make_async_copy(held, dst, sem.at[1, k])
+        for k, (held, dst) in enumerate(((u, x), (v, y), (w, z)))
+    ]
+    for copy in loads:
+        copy.start()
+    for load, store in zip(loads, stores):
+        load.wait()
+        store.start()
+    for copy in stores:
+        copy.wait()
 
 
 def body(tokens, row_cotangent, routes, w_gate, w_up):
@@ -450,35 +509,35 @@
     hbm = pl.BlockSpec(memory_space=pl.ANY)
     cols = width // n_dp
     dma = pltpu.SemaphoreType.DMA
-    gt, gg, gu = pl.pallas_call(
+    grads = pl.pallas_call(
         functools.partial(expert_kernel, (n_dp, n_ex, slots, tok, top)),
         out_shape=(
             jax.ShapeDtypeStruct((tok, width), BF16),
             jax.ShapeDtypeStruct((cols, hidden), F32),
             jax.ShapeDtypeStruct((cols, hidden), F32),
         ),
-        in_specs=[vmem, vmem, hbm, hbm, hbm, hbm],
+        in_specs=[vmem, hbm, hbm, hbm, hbm],
         out_specs=(vmem, vmem, vmem),
         scratch_shapes=[
             pltpu.VMEM((2, width, hidden), BF16),
             pltpu.VMEM((rows, 2 * hidden), BF16),
-            pltpu.VMEM((2, n_dp, cols, hidden), BF16),
-            pltpu.VMEM((2, cols, hidden), F32),
+            pltpu.VMEM((2, n_dp, 3, cols, hidden // 3), BF16),
+            pltpu.VMEM((2, 3, cols, hidden // 3), F32),
             pltpu.VMEM((n_ex, 2 * slots, width // 2), BF16),
             pltpu.VMEM((n_ex, 2 * slots, width // 2), BF16),
             pltpu.VMEM((2 * tok, 2 * rows), BF16),
             pltpu.VMEM((flat, hidden), BF16),
             pltpu.VMEM((n_ex // 2, 2, 2 * tok, width // 2), BF16),
             pltpu.VMEM((rows, width), BF16),
-            pltpu.VMEM((rows, hidden), BF16),
-            pltpu.VMEM((n_ex, 2 * slots, hidden // 2), BF16),
-            pltpu.VMEM((n_ex, 2 * slots, hidden // 2), BF16),
-            pltpu.VMEM((n_ex, 1, flat), jnp.int32),
+            pltpu.VMEM((2, rows, hidden // 3), F32),
+            pltpu.VMEM((n_ex, 6 * slots, hidden // 6), BF16),
+            pltpu.VMEM((n_ex, 6 * slots, hidden // 6), BF16),
+            pltpu.VMEM((n_ex, 1, flat), F32),
             pltpu.VMEM((n_ex, flat), F32),
             pltpu.VMEM((n_ex // 2, 2 * slots, 2 * tok), BF16),
             dma((2,)),
-            dma((2, n_dp, 2)),
-            dma((2, n_dp, 2)),
+            dma((2, n_dp, 3)),
+            dma((2, n_dp, 3)),
             dma((n_ex,)),
             dma((n_ex,)),
             dma,
@@ -487,8 +546,8 @@
             dma((2, SIDE * SIDE, 2)),
             dma((2, SIDE * SIDE)),
             dma((2, SIDE * SIDE)),
-            dma((n_ex,)),
-            dma((n_ex,)),
+            dma((2, n_ex)),
+            dma((2, n_ex)),
             dma((n_ex,)),
             dma((n_ex,)),
         ],
@@ -497,9 +556,16 @@
         ),
         name="expert_backward",
     )(
-        routes.reshape(1, flat), routes.reshape(flat, 1), tokens,
-        row_cotangent.reshape(flat, hidden), w_gate[0], w_up[0],
+        routes.T, tokens, row_cotangent.reshape(flat, hidden), w_gate[0], w_up[0],
     )
+    gt, gg, gu = pl.pallas_call(
+        hand_over,
+        out_shape=tuple(jax.ShapeDtypeStruct(g.shape, g.dtype) for g in grads),
+        in_specs=[hbm] * 3,
+        out_specs=[hbm] * 3,
+        scratch_shapes=[pltpu.VMEM(g.shape, g.dtype) for g in grads] + [dma((2, 3))],
+        name="hand_over",
+    )(*grads)
     return gt, gg[None], gu[None]
 
 

time: 134 us -> 120 us (0.90)
  local copies, waits for them, and re-layouts: 8.07 us -> 0 us
  Pallas kernels: 125 us -> 119 us
    pallas_call x1, Pallas kernels: 125 us -> 117 us  [body(): pl.pallas_call(functools.partial(expert_kernel, (n_dp, n_ex, slots, tok,...]
    unnamed x4 -> x0, local copies, waits for them, and re-layouts: 6.57 us -> none
    pallas_call x0 -> x1, Pallas kernels: none -> 2.41 us  [body(): pl.pallas_call(hand_over, out_shape=tuple((jax.ShapeDtypeStruct(g.shape,...]
    reshape x2 -> x0, local copies, waits for them, and re-layouts: 1.5 us -> none  [the longest x1 0.83 us: body(): routes.reshape(flat, 1)]
where the time goes in v4:
time: 120 us
  Pallas kernels  119 us (99%)
    pallas_call x1, Pallas kernels, body(): pl.pallas_call(functools.partial(expert_kernel, (n_dp, n_ex, slots, tok,...  117 us
    pallas_call x1, Pallas kernels, body(): pl.pallas_call(hand_over, out_shape=tuple((jax.ShapeDtypeStruct(g.shape,...  2.41 us

profile of v4, /device:TPU:1, one launch (start us, length us, event | category | flops | bytes accessed | tf_op | source)
XLA Modules:
  0.0 120.1 jit_solution(13220195723763241154)
XLA Ops:
  0.6 116.9 %expert_backward.1 = (bf16[64,2048]{1,0:T(8,128)(2,1)}, f32[256,768]{1,0:T(8,128)}, f32[256,768]{1,0:T(8,128)}) custom-call(s32[8,64]{1,0:T(8,128)} %bitcast.9, bf16[64,2048]{1,0:T(8,128)(2,1)} %x_hbm.1, bf16[512,768]{1,0:T(8,128)(2,1)} %bitcast.8, bf16[2048,768]{1,0:T(8,128)(2,1)} %bitcast.6, bf16[2048,768]{1,0:T(8,128)(2,1)} %bitcast.7), custom_call_target="tpu_custom_call" | custom-call | tf_op jit(solution)/shard_map/expert_backward/pallas_call | solution.py:512
  117.5 2.4 %hand_over.1 = (bf16[64,2048]{1,0:T(8,128)(2,1)}, f32[256,768]{1,0:T(8,128)}, f32[256,768]{1,0:T(8,128)}) custom-call(bf16[64,2048]{1,0:T(8,128)(2,1)} %get-tuple-element.9.a, f32[256,768]{1,0:T(8,128)} %get-tuple-element.10.b, f32[256,768]{1,0:T(8,128)} %get-tuple-element.11.c), custom_call_target="tpu_custom_call" | custom-call | tf_op jit(solution)/shard_map/hand_over/pallas_call | solution.py:561

commit v5 on v4

--- a/solution.py
+++ b/solution.py
@@ -22,7 +22,8 @@
     gt_ref, gg_ref, gu_ref,
     w_ref, d_ref, ring_ref, part_ref, back_ref, ret_ref, comb_ref,
     cot_ref, xg_ref, xs_ref, gate_ref, dh_out, dh_in, all_ref, flat_ref, sel_ref,
-    w_sem, ring_send, ring_recv, ret_send, ret_recv, own_sem,
+    mine_ref, gt_buf, g_buf,
+    w_sem, ring_send, ring_recv, ret_send, ret_recv, out_sem,
     in_sem, ag_send, ag_recv, sib_send, sib_recv, dh_send, dh_recv, r_send, r_recv,
 ):
     n_dp, n_ex, slots, tok, top = dims
@@ -62,6 +63,114 @@
 
     lax.fori_loop(1, n_ex, greet, 0)
 
+    for c in loads[:2]:
+        c.wait()
+
+    def chip_at(h, da, db):
+        dx, dy = (da, db) if h == 0 else (db, da)
+        return lax.rem(my + dy, SIDE) * SIDE + lax.rem(mx + dx, SIDE)
+
+    def off(da, db):
+        return (da % SIDE) * SIDE + db % SIDE
+
+    def slab(h, da, db, lo, n, of_core):
+        return xg_ref.at[
+            chip_at(h, da % SIDE, db % SIDE), h,
+            pl.ds(pl.multiple_of(of_core * tok + lo, tok // 2), n),
+        ]
+
+    sends = []
+
+    def pass_on(h, da, db, axis, sign, piece=None):
+        lo, n = (0, tok) if piece is None else (piece * (tok // 2), tok // 2)
+        ra, rb = (da - sign, db) if axis == 0 else (da, db - sign)
+        ta, tb = (sign % SIDE, 0) if axis == 0 else (0, sign % SIDE)
+        ref = slab(h, da, db, lo, n, core)
+        c = pltpu.make_async_remote_copy(
+            src_ref=ref, dst_ref=ref,
+            send_sem=ag_send.at[len(sends)],
+            recv_sem=ag_recv.at[h, off(ra, rb), piece or 0],
+            device_id={"expert": chip_at(h, ta, tb) * 2 + core},
+            device_id_type=MESH,
+        )
+        c.start()
+        sends.append(c)
+
+    def arrived(h, da, db, piece=None):
+        lo, n = (0, tok) if piece is None else (piece * (tok // 2), tok // 2)
+        ref = slab(h, da, db, lo, n, core)
+        pltpu.make_async_remote_copy(
+            src_ref=ref, dst_ref=ref, send_sem=ag_send.at[0],
+            recv_sem=ag_recv.at[h, off(da, db), piece or 0],
+            device_id={"expert": me}, device_id_type=MESH,
+        ).wait_recv()
+
+    def sibling(h, da, db, of_core):
+        ref = slab(h, da, db, 0, tok, of_core)
+        return pltpu.make_async_remote_copy(
+            src_ref=ref, dst_ref=ref,
+            send_sem=sib_send.at[h, off(da, db)],
+            recv_sem=sib_recv.at[h, off(da, db)],
+            device_id={"expert": me + 1 - 2 * core},
+            device_id_type=MESH,
+        )
+
+    def share(h, da, db):
+        sibling(h, da, db, core).start()
+
+    def select(h, da, db):
+        sibling(h, da, db, 1 - core).wait_recv()
+        chip = chip_at(h, da % SIDE, db % SIDE)
+        xs_ref[
+            pl.ds(pl.multiple_of(chip * 2 * slots, 2 * slots), 2 * slots),
+            h * half_w:(h + 1) * half_w,
+        ] = jnp.dot(sel_ref[chip], xg_ref[chip, h], preferred_element_type=F32).astype(BF16)
+
+    def route_copy(t, slot):
+        return pltpu.make_async_remote_copy(
+            src_ref=mine_ref, dst_ref=all_ref.at[slot],
+            send_sem=r_send, recv_sem=r_recv,
+            device_id={"expert": t}, device_id_type=MESH,
+        )
+
+    def dh_piece(ref, q):
+        lanes = pl.ds(q * 2 * slots, 2 * (q + 1) * slots)
+        return ref.at[:, lanes] if len(ref.shape) == 3 else ref.at[lanes]
+
+    def dh_copy(t, slot, q):
+        return pltpu.make_async_remote_copy(
+            src_ref=dh_piece(dh_out.at[t], q), dst_ref=dh_piece(dh_in.at[slot], q),
+            send_sem=dh_send.at[q], recv_sem=dh_recv.at[q],
+            device_id={"expert": t}, device_id_type=MESH,
+        )
+
+    def landed(ref, sem):
+        pltpu.make_async_copy(ref, ref, sem).wait()
+
+    def keep_own(own, to, sem):
+        pltpu.make_async_copy(own, to, sem).start()
+
+    def peers(go):
+        def one(k, c):
+            go(lax.rem(me + k, n_ex))
+            return c
+
+        lax.fori_loop(1, n_ex, one, 0)
+
+    def to_peers(go):
+        for dx, dy in ROUND:
+            for dc in range(2):
+                go(chip_at(0, dx, dy) * 2 + lax.rem(core + dc, 2))
+        go(me + 1 - 2 * core)
+
+    pl.semaphore_wait(barrier, n_ex + 1)
+    for h in range(2):
+        for sign in (1, -1):
+            pass_on(h, 0, 0, 0, sign)
+    for h in range(2):
+        for sign in (1, -1):
+            pass_on(h, 0, 0, 1, sign)
+        share(h, 0, 0)
     flat = tok * top
     early = lax.broadcasted_iota(jnp.int32, (flat, flat), 0)
     late = lax.broadcasted_iota(jnp.int32, (flat, flat), 1)
@@ -78,6 +187,9 @@
     at_col = lax.rem(lax.broadcasted_iota(jnp.int32, (flat, top), 0), top)
     route_row = jnp.sum(jnp.where(j_row == at_row, by_row, 0.0), axis=0, keepdims=True)
     route_col = jnp.sum(jnp.where(j_col == at_col, by_col, 0.0), axis=1, keepdims=True)
+    mine_ref[...] = route_row
+    peers(lambda t: route_copy(t, me).start())
+    keep_own(mine_ref, all_ref.at[me], r_recv)
     same = route_col == route_row
     rank_row = jnp.sum(jnp.where(same & (early < late), 1.0, 0.0), axis=0, keepdims=True)
     rank_col = jnp.sum(jnp.where(same & (late < early), 1.0, 0.0), axis=1, keepdims=True)
@@ -93,13 +205,6 @@
     pos_col = placed(route_col, rank_col, 2 * slots)
 
     wide = 2 * n_ex * slots
-    place = lax.broadcasted_iota(jnp.int32, (flat, wide), 1)
-    for k in range(2):
-        hit = jnp.where(place == pos_col + k * slots, 1.0, 0.0).astype(BF16)
-        comb_ref[k * tok:(k + 1) * tok, :] = jnp.dot(
-            group, hit, preferred_element_type=F32
-        ).astype(BF16)
-
     lot = 8
     loads[2].wait()
 
@@ -115,110 +220,8 @@
         return c
 
     lax.fori_loop(0, n_ex // lot, pack, 0)
-    all_ref[me] = route_row
-    for c in loads[:2]:
-        c.wait()
-
-    def chip_at(h, da, db):
-        dx, dy = (da, db) if h == 0 else (db, da)
-        return lax.rem(my + dy, SIDE) * SIDE + lax.rem(mx + dx, SIDE)
-
-    def off(da, db):
-        return (da % SIDE) * SIDE + db % SIDE
-
-    def slab(h, da, db, lo, n, of_core):
-        return xg_ref.at[
-            chip_at(h, da % SIDE, db % SIDE), h,
-            pl.ds(pl.multiple_of(of_core * tok + lo, tok // 2), n),
-        ]
-
-    sends = []
-
-    def pass_on(h, da, db, axis, sign, piece=None):
-        lo, n = (0, tok) if piece is None else (piece * (tok // 2), tok // 2)
-        ra, rb = (da - sign, db) if axis == 0 else (da, db - sign)
-        ta, tb = (sign % SIDE, 0) if axis == 0 else (0, sign % SIDE)
-        ref = slab(h, da, db, lo, n, core)
-        c = pltpu.make_async_remote_copy(
-            src_ref=ref, dst_ref=ref,
-            send_sem=ag_send.at[len(sends)],
-            recv_sem=ag_recv.at[h, off(ra, rb), piece or 0],
-            device_id={"expert": chip_at(h, ta, tb) * 2 + core},
-            device_id_type=MESH,
-        )
-        c.start()
-        sends.append(c)
-
-    def arrived(h, da, db, piece=None):
-        lo, n = (0, tok) if piece is None else (piece * (tok // 2), tok // 2)
-        ref = slab(h, da, db, lo, n, core)
-        pltpu.make_async_remote_copy(
-            src_ref=ref, dst_ref=ref, send_sem=ag_send.at[0],
-            recv_sem=ag_recv.at[h, off(da, db), piece or 0],
-            device_id={"expert": me}, device_id_type=MESH,
-        ).wait_recv()
-
-    def sibling(h, da, db, of_core):
-        ref = slab(h, da, db, 0, tok, of_core)
-        return pltpu.make_async_remote_copy(
-            src_ref=ref, dst_ref=ref,
-            send_sem=sib_send.at[h, off(da, db)],
-            recv_sem=sib_recv.at[h, off(da, db)],
-            device_id={"expert": me + 1 - 2 * core},
-            device_id_type=MESH,
-        )
-
-    def share(h, da, db):
-        sibling(h, da, db, core).start()
-
-    def select(h, da, db):
-        sibling(h, da, db, 1 - core).wait_recv()
-        chip = chip_at(h, da % SIDE, db % SIDE)
-        xs_ref[
-            pl.ds(pl.multiple_of(chip * 2 * slots, 2 * slots), 2 * slots),
-            h * half_w:(h + 1) * half_w,
-        ] = jnp.dot(sel_ref[chip], xg_ref[chip, h], preferred_element_type=F32).astype(BF16)
-
-    def route_copy(t, slot):
-        return pltpu.make_async_remote_copy(
-            src_ref=all_ref.at[me], dst_ref=all_ref.at[slot],
-            send_sem=r_send.at[t], recv_sem=r_recv.at[slot],
-            device_id={"expert": t}, device_id_type=MESH,
-        )
-
-    def dh_piece(ref, q):
-        return ref.at[pl.ds(q * 2 * slots, 2 * (q + 1) * slots)]
-
-    def dh_copy(t, slot, q):
-        return pltpu.make_async_remote_copy(
-            src_ref=dh_piece(dh_out.at[t], q), dst_ref=dh_piece(dh_in.at[slot], q),
-            send_sem=dh_send.at[q, t], recv_sem=dh_recv.at[q, slot],
-            device_id={"expert": t}, device_id_type=MESH,
-        )
-
-    def peers(go):
-        def one(k, c):
-            go(lax.rem(me + k, n_ex))
-            return c
-
-        lax.fori_loop(1, n_ex, one, 0)
-
-    def to_peers(go):
-        for dx, dy in ROUND:
-            for dc in range(2):
-                go(chip_at(0, dx, dy) * 2 + lax.rem(core + dc, 2))
-        go(me + 1 - 2 * core)
-
-    pl.semaphore_wait(barrier, n_ex + 1)
-    for h in range(2):
-        for sign in (1, -1):
-            pass_on(h, 0, 0, 0, sign)
-    peers(lambda t: route_copy(t, me).start())
-    for h in range(2):
-        for sign in (1, -1):
-            pass_on(h, 0, 0, 1, sign)
-        share(h, 0, 0)
     to_peers(lambda t: dh_copy(t, me, 0).start())
+    keep_own(dh_piece(dh_out.at[me], 0), dh_piece(dh_in.at[me], 0), dh_recv.at[0])
 
     both_ways = [(h, sign) for h in range(2) for sign in (1, -1)]
     for h, sign in both_ways:
@@ -239,7 +242,7 @@
             pass_on(h, 2, 0, 1, sign)
         share(h, 2, 0)
 
-    peers(lambda t: route_copy(t, t).wait())
+    landed(all_ref, r_recv)
     for s in range(n_ex):
         flat_ref[s:s + 1, :] = all_ref[s]
     named = flat_ref[...]
@@ -285,8 +288,8 @@
             arrived(h, da, -sign)
             pass_on(h, da, -sign, 1, sign, 0 if sign == 1 else 1)
             share(h, da, -sign)
-    dh_own = pltpu.make_async_copy(dh_out.at[me], dh_in.at[me], in_sem.at[3])
-    dh_own.start()
+    to_peers(lambda t: dh_copy(t, me, 1).start())
+    keep_own(dh_piece(dh_out.at[me], 1), dh_piece(dh_in.at[me], 1), dh_recv.at[1])
     for h in range(2):
         for da, db in ((0, 1), (0, -1), (2, 0), (1, 1), (1, -1), (-1, 1), (-1, -1)):
             select(h, da, db)
@@ -295,7 +298,6 @@
             for piece in range(2):
                 arrived(h, da, 2, piece)
             share(h, da, 2)
-    to_peers(lambda t: dh_copy(t, me, 1).start())
     for h in range(2):
         for da, db in ((2, 1), (2, -1), (0, 2), (1, 2), (-1, 2), (2, 2)):
             select(h, da, db)
@@ -354,11 +356,8 @@
 
     def begin(b):
         gates(b)
-        if b == 0:
-            peers(lambda t: dh_copy(t, t, 0).wait())
-            dh_own.wait()
-        if b == 1:
-            peers(lambda t: dh_copy(t, t, 1).wait())
+        if b < 2:
+            landed(dh_piece(dh_in, b), dh_recv.at[b])
         cotangents(b)
         for k in range(2):
             ring_ref[k, 0, b] = part(chunk(0, k), k, b).astype(BF16)
@@ -400,17 +399,15 @@
         return pltpu.make_async_remote_copy(
             src_ref=back_ref.at[t],
             dst_ref=ret_ref.at[me],
-            send_sem=ret_send.at[t],
-            recv_sem=ret_recv.at[me],
+            send_sem=ret_send,
+            recv_sem=ret_recv,
             device_id={"expert": t},
             device_id_type=MESH,
         )
 
-    own_copy = pltpu.make_async_copy(back_ref.at[me], ret_ref.at[me], own_sem)
-
     def start_returns(i, y):
         if i == 0:
-            own_copy.start()
+            keep_own(back_ref.at[me], ret_ref.at[me], ret_recv)
         for dx in (1, 3, 0, 2):
             for dc in range(2):
                 if (i, dx, dc) != (0, 0, 0):
@@ -433,35 +430,39 @@
     start_returns(2, back_half(2, 1))
     unit(3, 2)
 
+    place = lax.broadcasted_iota(jnp.int32, (flat, wide), 1)
+    for k in range(2):
+        hit = jnp.where(place == pos_col + k * slots, 1.0, 0.0).astype(BF16)
+        comb_ref[k * tok:(k + 1) * tok, :] = jnp.dot(
+            group, hit, preferred_element_type=F32
+        ).astype(BF16)
+
     def alone(s, c):
         for b in range(3):
             unit(s, b)
         return c
 
     lax.fori_loop(4, n_dp - 1, alone, 0)
-    def got(j, c):
-        t = lax.rem(me + j, n_ex)
-        pltpu.make_async_remote_copy(
-            src_ref=back_ref.at[t], dst_ref=ret_ref.at[t], send_sem=ret_send.at[t],
-            recv_sem=ret_recv.at[t], device_id={"expert": t}, device_id_type=MESH,
-        ).wait()
-        return c
-
-    lax.fori_loop(1, n_ex, got, 0)
-    own_copy.wait()
+    landed(ret_ref, ret_recv)
     summed = jnp.dot(
         comb_ref[...], ret_ref[...].reshape(wide, wide_col), preferred_element_type=F32
     )
-    gt_ref[:, :wide_col] = summed[:tok].astype(BF16)
-    gt_ref[:, wide_col:] = summed[tok:].astype(BF16)
+    gt_buf[:, :wide_col] = summed[:tok].astype(BF16)
+    gt_buf[:, wide_col:] = summed[tok:].astype(BF16)
+    outs = [pltpu.make_async_copy(gt_buf, gt_ref, out_sem.at[6])]
+    outs[0].start()
 
     scale = 1.0 / n_dp
     for b in range(3):
         for k, out in enumerate((gg_ref, gu_ref)):
             ring_copy(n_dp - 2, k, b).wait_recv()
-            out[:, b * third:(b + 1) * third] = (
-                ring_ref[k, n_dp - 1, b].astype(F32) + part_ref[k, b]
-            ) * scale
+            g_buf[k, b] = (ring_ref[k, n_dp - 1, b].astype(F32) + part_ref[k, b]) * scale
+            outs.append(
+                pltpu.make_async_copy(
+                    g_buf.at[k, b], out.at[:, pl.ds(b * third, third)], out_sem.at[2 * b + k]
+                )
+            )
+            outs[-1].start()
 
     def sent(s, c):
         for k in range(2):
@@ -472,6 +473,13 @@
     lax.fori_loop(0, n_dp - 1, sent, 0)
     for c in sends:
         c.wait_send()
+    for c in outs:
+        c.wait()
+    others = pl.ds(0, n_ex - 1)
+    landed(all_ref.at[others], r_send)
+    landed(back_ref.at[others], ret_send)
+    for q in range(2):
+        landed(dh_piece(dh_out.at[others], q), dh_send.at[q])
     for h in range(2):
         for da in range(SIDE):
             for db in range(SIDE):
@@ -517,7 +525,7 @@
             jax.ShapeDtypeStruct((cols, hidden), F32),
         ),
         in_specs=[vmem, hbm, hbm, hbm, hbm],
-        out_specs=(vmem, vmem, vmem),
+        out_specs=(hbm, hbm, hbm),
         scratch_shapes=[
             pltpu.VMEM((2, width, hidden), BF16),
             pltpu.VMEM((rows, 2 * hidden), BF16),
@@ -535,21 +543,24 @@
             pltpu.VMEM((n_ex, 1, flat), F32),
             pltpu.VMEM((n_ex, flat), F32),
             pltpu.VMEM((n_ex // 2, 2 * slots, 2 * tok), BF16),
+            pltpu.VMEM((1, flat), F32),
+            pltpu.VMEM((tok, width), BF16),
+            pltpu.VMEM((2, 3, cols, hidden // 3), F32),
             dma((2,)),
             dma((2, n_dp, 3)),
             dma((2, n_dp, 3)),
-            dma((n_ex,)),
-            dma((n_ex,)),
             dma,
-            dma((4,)),
+            dma,
+            dma((7,)),
+            dma((3,)),
             dma((40,)),
             dma((2, SIDE * SIDE, 2)),
             dma((2, SIDE * SIDE)),
             dma((2, SIDE * SIDE)),
-            dma((2, n_ex)),
-            dma((2, n_ex)),
-            dma((n_ex,)),
-            dma((n_ex,)),
+            dma((2,)),
+            dma((2,)),
+            dma,
+            dma,
         ],
         compiler_params=pltpu.CompilerParams(
             collective_id=0, has_side_effects=True, vmem_limit_bytes=56 << 20

time: 120 us -> 115 us (0.958)
  Pallas kernels: 119 us -> 114 us
    pallas_call x1, Pallas kernels: 117 us -> 111 us  [body(): pl.pallas_call(functools.partial(expert_kernel, (n_dp, n_ex, slots, tok,...]
where the time goes in v5:
time: 115 us
  Pallas kernels  114 us (99%)
    pallas_call x1, Pallas kernels, body(): pl.pallas_call(functools.partial(expert_kernel, (n_dp, n_ex, slots, tok,...  111 us
    pallas_call x1, Pallas kernels, body(): pl.pallas_call(hand_over, out_shape=tuple((jax.ShapeDtypeStruct(g.shape,...  2.41 us

profile of v5, /device:TPU:1, one launch (start us, length us, event | category | flops | bytes accessed | tf_op | source)
XLA Modules:
  0.0 114.6 jit_solution(7296458485016903926)
XLA Ops:
  0.6 111.4 %expert_backward.1 = (bf16[64,2048]{1,0:T(8,128)(2,1)}, f32[256,768]{1,0:T(8,128)}, f32[256,768]{1,0:T(8,128)}) custom-call(s32[8,64]{1,0:T(8,128)} %bitcast.9, bf16[64,2048]{1,0:T(8,128)(2,1)} %x_hbm.1, bf16[512,768]{1,0:T(8,128)(2,1)} %bitcast.8, bf16[2048,768]{1,0:T(8,128)(2,1)} %bitcast.6, bf16[2048,768]{1,0:T(8,128)(2,1)} %bitcast.7), custom_call_target="tpu_custom_call" | custom-call | tf_op jit(solution)/shard_map/expert_backward/pallas_call | solution.py:520
  112.0 2.4 %hand_over.1 = (bf16[64,2048]{1,0:T(8,128)(2,1)}, f32[256,768]{1,0:T(8,128)}, f32[256,768]{1,0:T(8,128)}) custom-call(bf16[64,2048]{1,0:T(8,128)(2,1)} %get-tuple-element.9.a, f32[256,768]{1,0:T(8,128)} %get-tuple-element.10.b, f32[256,768]{1,0:T(8,128)} %get-tuple-element.11.c), custom_call_target="tpu_custom_call" | custom-call | tf_op jit(solution)/shard_map/hand_over/pallas_call | solution.py:572

commit v6 on v5

--- a/solution.py
+++ b/solution.py
@@ -18,11 +18,11 @@
 
 def expert_kernel(
     dims,
-    routes_ref, x_hbm, cot_hbm, wg_hbm, wu_hbm,
+    routes_hbm, x_hbm, cot_hbm, wg_hbm, wu_hbm,
     gt_ref, gg_ref, gu_ref,
     w_ref, d_ref, ring_ref, part_ref, back_ref, ret_ref, comb_ref,
     cot_ref, xg_ref, xs_ref, gate_ref, dh_out, dh_in, all_ref, flat_ref, sel_ref,
-    mine_ref, gt_buf, g_buf,
+    routes_ref, mine_ref, gt_buf, g_buf,
     w_sem, ring_send, ring_recv, ret_send, ret_recv, out_sem,
     in_sem, ag_send, ag_recv, sib_send, sib_recv, dh_send, dh_recv, r_send, r_recv,
 ):
@@ -34,6 +34,19 @@
     lane = third // 2
     me = lax.axis_index("expert")
     p = lax.axis_index("dp")
+    barrier = pltpu.get_barrier_semaphore()
+    right, left = lax.rem(p + 1, n_dp), lax.rem(p + n_dp - 1, n_dp)
+    for z in (left, right):
+        pl.semaphore_signal(barrier, inc=1, device_id={"dp": z}, device_id_type=MESH)
+
+    def greet(k, c):
+        pl.semaphore_signal(
+            barrier, inc=1, device_id={"expert": lax.rem(me + k, n_ex)}, device_id_type=MESH
+        )
+        return c
+
+    lax.fori_loop(1, n_ex, greet, 0)
+
     core = lax.rem(me, 2)
     mx, my = lax.rem(me // 2, SIDE), me // (2 * SIDE)
     half_w = width // 2
@@ -43,25 +56,16 @@
             x_hbm.at[:, pl.ds(h * half_w, half_w)], xg_ref.at[me // 2, h, own_rows], in_sem.at[h]
         )
         for h in range(2)
-    ] + [pltpu.make_async_copy(cot_hbm, cot_ref, in_sem.at[2])]
+    ] + [
+        pltpu.make_async_copy(cot_hbm, cot_ref, in_sem.at[2]),
+        pltpu.make_async_copy(routes_hbm, routes_ref, in_sem.at[3]),
+    ]
     w_copies = [
         pltpu.make_async_copy(src, w_ref.at[k], w_sem.at[k])
         for k, src in enumerate((wg_hbm, wu_hbm))
     ]
     for c in loads + w_copies:
         c.start()
-    barrier = pltpu.get_barrier_semaphore()
-    right, left = lax.rem(p + 1, n_dp), lax.rem(p + n_dp - 1, n_dp)
-    for z in (left, right):
-        pl.semaphore_signal(barrier, inc=1, device_id={"dp": z}, device_id_type=MESH)
-
-    def greet(k, c):
-        pl.semaphore_signal(
-            barrier, inc=1, device_id={"expert": lax.rem(me + k, n_ex)}, device_id_type=MESH
-        )
-        return c
-
-    lax.fori_loop(1, n_ex, greet, 0)
 
     for c in loads[:2]:
         c.wait()
@@ -78,8 +82,6 @@
             chip_at(h, da % SIDE, db % SIDE), h,
             pl.ds(pl.multiple_of(of_core * tok + lo, tok // 2), n),
         ]
-
-    sends = []
 
     def pass_on(h, da, db, axis, sign, piece=None):
         lo, n = (0, tok) if piece is None else (piece * (tok // 2), tok // 2)
@@ -88,19 +90,18 @@
         ref = slab(h, da, db, lo, n, core)
         c = pltpu.make_async_remote_copy(
             src_ref=ref, dst_ref=ref,
-            send_sem=ag_send.at[len(sends)],
+            send_sem=ag_send,
             recv_sem=ag_recv.at[h, off(ra, rb), piece or 0],
             device_id={"expert": chip_at(h, ta, tb) * 2 + core},
             device_id_type=MESH,
         )
         c.start()
-        sends.append(c)
 
     def arrived(h, da, db, piece=None):
         lo, n = (0, tok) if piece is None else (piece * (tok // 2), tok // 2)
         ref = slab(h, da, db, lo, n, core)
         pltpu.make_async_remote_copy(
-            src_ref=ref, dst_ref=ref, send_sem=ag_send.at[0],
+            src_ref=ref, dst_ref=ref, send_sem=ag_send,
             recv_sem=ag_recv.at[h, off(da, db), piece or 0],
             device_id={"expert": me}, device_id_type=MESH,
         ).wait_recv()
@@ -109,7 +110,7 @@
         ref = slab(h, da, db, 0, tok, of_core)
         return pltpu.make_async_remote_copy(
             src_ref=ref, dst_ref=ref,
-            send_sem=sib_send.at[h, off(da, db)],
+            send_sem=sib_send,
             recv_sem=sib_recv.at[h, off(da, db)],
             device_id={"expert": me + 1 - 2 * core},
             device_id_type=MESH,
@@ -177,6 +178,7 @@
     row_of = lax.broadcasted_iota(jnp.int32, (tok, flat), 1)
     token_of = lax.broadcasted_iota(jnp.int32, (tok, flat), 0) * top
     group = jnp.where((row_of >= token_of) & (row_of < token_of + top), 1.0, 0.0).astype(BF16)
+    loads[3].wait()
     named = routes_ref[...].astype(F32).astype(BF16)
     over_first = (((0,), (0,)), ((), ()))
     by_row = jnp.dot(named, group, preferred_element_type=F32)
@@ -293,26 +295,21 @@
     for h in range(2):
         for da, db in ((0, 1), (0, -1), (2, 0), (1, 1), (1, -1), (-1, 1), (-1, -1)):
             select(h, da, db)
-    for da in (0, 1, -1, 2):
-        for h in range(2):
-            for piece in range(2):
-                arrived(h, da, 2, piece)
-            share(h, da, 2)
-    for h in range(2):
-        for da, db in ((2, 1), (2, -1), (0, 2), (1, 2), (-1, 2), (2, 2)):
-            select(h, da, db)
     for c in w_copies:
         c.wait()
     m_blk = rows // 2
 
+    def gate_block(b, at, n):
+        r = pl.ds(pl.multiple_of(at, n), n)
+        for k in range(2):
+            gate_ref[k, r] = jnp.dot(
+                xs_ref[r, :], w_ref[k, :, b * third:(b + 1) * third],
+                preferred_element_type=F32,
+            )
+
     def gates(b):
         def one(i, c):
-            r = pl.ds(pl.multiple_of(i * m_blk, m_blk), m_blk)
-            for k in range(2):
-                gate_ref[k, r] = jnp.dot(
-                    xs_ref[r, :], w_ref[k, :, b * third:(b + 1) * third],
-                    preferred_element_type=F32,
-                )
+            gate_block(b, i * m_blk, m_blk)
             return c
 
         lax.fori_loop(0, 2, one, 0)
@@ -348,14 +345,15 @@
         return pltpu.make_async_remote_copy(
             src_ref=ring_ref.at[k, s, b],
             dst_ref=ring_ref.at[k, s + 1, b],
-            send_sem=ring_send.at[k, s, b],
+            send_sem=ring_send,
             recv_sem=ring_recv.at[k, s, b],
             device_id={"dp": right if k == 0 else left},
             device_id_type=MESH,
         )
 
     def begin(b):
-        gates(b)
+        if b:
+            gates(b)
         if b < 2:
             landed(dh_piece(dh_in, b), dh_recv.at[b])
         cotangents(b)
@@ -373,6 +371,29 @@
         for k in range(2):
             part_ref[k, b] = part(chunk(s + 1, k), k, b)
 
+    y_blk = SIDE * 2 * slots
+
+    def first_gates(dy):
+        gate_block(0, lax.rem(my + dy, SIDE) * y_blk, y_blk)
+
+    for da in (0, 1, -1):
+        for h in range(2):
+            for piece in range(2):
+                arrived(h, da, 2, piece)
+            share(h, da, 2)
+    for h in range(2):
+        for da, db in ((2, 1), (2, -1), (0, 2), (1, 2), (-1, 2)):
+            select(h, da, db)
+    first_gates(0)
+    for h in range(2):
+        for piece in range(2):
+            arrived(h, 2, 2, piece)
+        share(h, 2, 2)
+    first_gates(1)
+    first_gates(3)
+    for h in range(2):
+        select(h, 2, 2)
+    first_gates(2)
     begin(0)
     begin(1)
     unit(1, 0)
@@ -464,26 +485,16 @@
             )
             outs[-1].start()
 
-    def sent(s, c):
-        for k in range(2):
-            for b in range(3):
-                ring_copy(s, k, b).wait_send()
-        return c
-
-    lax.fori_loop(0, n_dp - 1, sent, 0)
-    for c in sends:
-        c.wait_send()
     for c in outs:
         c.wait()
+    landed(ring_ref.at[:, pl.ds(0, n_dp - 1)], ring_send)
+    landed(xg_ref.at[pl.ds(0, n_ex // 2 - 1), 0], ag_send)
+    landed(xg_ref.at[:, 0], sib_send)
     others = pl.ds(0, n_ex - 1)
     landed(all_ref.at[others], r_send)
     landed(back_ref.at[others], ret_send)
     for q in range(2):
         landed(dh_piece(dh_out.at[others], q), dh_send.at[q])
-    for h in range(2):
-        for da in range(SIDE):
-            for db in range(SIDE):
-                sibling(h, da, db, core).wait_send()
 
 
 def hand_over(a, b, c, x, y, z, u, v, w, sem):
@@ -524,7 +535,7 @@
             jax.ShapeDtypeStruct((cols, hidden), F32),
             jax.ShapeDtypeStruct((cols, hidden), F32),
         ),
-        in_specs=[vmem, hbm, hbm, hbm, hbm],
+        in_specs=[hbm] * 5,
         out_specs=(hbm, hbm, hbm),
         scratch_shapes=[
             pltpu.VMEM((2, width, hidden), BF16),
@@ -543,19 +554,20 @@
             pltpu.VMEM((n_ex, 1, flat), F32),
             pltpu.VMEM((n_ex, flat), F32),
             pltpu.VMEM((n_ex // 2, 2 * slots, 2 * tok), BF16),
+            pltpu.VMEM((top, tok), jnp.int32),
             pltpu.VMEM((1, flat), F32),
             pltpu.VMEM((tok, width), BF16),
             pltpu.VMEM((2, 3, cols, hidden // 3), F32),
             dma((2,)),
-            dma((2, n_dp, 3)),
+            dma,
             dma((2, n_dp, 3)),
             dma,
             dma,
             dma((7,)),
-            dma((3,)),
-            dma((40,)),
+            dma((4,)),
+            dma,
             dma((2, SIDE * SIDE, 2)),
-            dma((2, SIDE * SIDE)),
+            dma,
             dma((2, SIDE * SIDE)),
             dma((2,)),
             dma((2,)),

time: 115 us -> 113 us (0.983)
  Pallas kernels: 114 us -> 112 us
    pallas_call x1, Pallas kernels: 111 us -> 110 us  [body(): pl.pallas_call(functools.partial(expert_kernel, (n_dp, n_ex, slots, tok,...]
where the time goes in v6:
time: 113 us
  Pallas kernels  112 us (99%)
    pallas_call x1, Pallas kernels, body(): pl.pallas_call(functools.partial(expert_kernel, (n_dp, n_ex, slots, tok,...  110 us
    pallas_call x1, Pallas kernels, body(): pl.pallas_call(hand_over, out_shape=tuple((jax.ShapeDtypeStruct(g.shape,...  2.41 us

profile of v6, /device:TPU:1, one launch (start us, length us, event | category | flops | bytes accessed | tf_op | source)
XLA Modules:
  0.0 113.0 jit_solution(16687593864585957998)
XLA Ops:
  0.6 109.8 %expert_backward.1 = (bf16[64,2048]{1,0:T(8,128)(2,1)}, f32[256,768]{1,0:T(8,128)}, f32[256,768]{1,0:T(8,128)}) custom-call(s32[8,64]{1,0:T(8,128)} %bitcast.9, bf16[64,2048]{1,0:T(8,128)(2,1)} %x_hbm.1, bf16[512,768]{1,0:T(8,128)(2,1)} %bitcast.8, bf16[2048,768]{1,0:T(8,128)(2,1)} %bitcast.6, bf16[2048,768]{1,0:T(8,128)(2,1)} %bitcast.7), custom_call_target="tpu_custom_call" | custom-call | tf_op jit(solution)/shard_map/expert_backward/pallas_call | solution.py:531
  110.4 2.4 %hand_over.1 = (bf16[64,2048]{1,0:T(8,128)(2,1)}, f32[256,768]{1,0:T(8,128)}, f32[256,768]{1,0:T(8,128)}) custom-call(bf16[64,2048]{1,0:T(8,128)(2,1)} %get-tuple-element.9.a, f32[256,768]{1,0:T(8,128)} %get-tuple-element.10.b, f32[256,768]{1,0:T(8,128)} %get-tuple-element.11.c), custom_call_target="tpu_custom_call" | custom-call | tf_op jit(solution)/shard_map/hand_over/pallas_call | solution.py:584

commit v7 on v6

--- a/solution.py
+++ b/solution.py
@@ -215,10 +215,11 @@
         hit = jnp.where(spot == pos_row, 1.0, 0.0).astype(BF16)
         v = jnp.dot(hit, cot_ref[...], preferred_element_type=F32).reshape(lot, slots, hidden)
         for j in range(lot):
-            for k in range(6):
-                dh_out[i * lot + j, k * slots:(k + 1) * slots, :] = v[
-                    j, :, k * lane:(k + 1) * lane
-                ].astype(BF16)
+            for b in range(3):
+                both = [v[j, :, k * lane:(k + 1) * lane] for k in (2 * b, 2 * b + 1)]
+                dh_out[i * lot + j, 2 * b * slots:2 * (b + 1) * slots, :] = jnp.concatenate(
+                    both, axis=0
+                ).astype(BF16)
         return c
 
     lax.fori_loop(0, n_ex // lot, pack, 0)
@@ -352,7 +353,7 @@
         )
 
     def begin(b):
-        if b:
+        if b == 2:
             gates(b)
         if b < 2:
             landed(dh_piece(dh_in, b), dh_recv.at[b])
@@ -395,9 +396,11 @@
         select(h, 2, 2)
     first_gates(2)
     begin(0)
+    gates(1)
+    unit(1, 0)
     begin(1)
-    unit(1, 0)
     begin(2)
+    unit(2, 0)
     side = 8
     wide_col = width // 2
 
@@ -439,7 +442,6 @@
     start_returns(0, back_half(0, 1))
     unit(1, 2)
     back_half(1, 0)
-    unit(2, 0)
     start_returns(1, back_half(1, 1))
     unit(2, 1)
     back_half(3, 0)

time: 113 us -> 112 us (level)
  no operation moved by 1% of the time
where the time goes in v7:
time: 112 us
  Pallas kernels  112 us (100%)
    pallas_call x1, Pallas kernels, body(): pl.pallas_call(functools.partial(expert_kernel, (n_dp, n_ex, slots, tok,...  109 us
    pallas_call x1, Pallas kernels, body(): pl.pallas_call(hand_over, out_shape=tuple((jax.ShapeDtypeStruct(g.shape,...  2.41 us

profile of v7, /device:TPU:1, one launch (start us, length us, event | category | flops | bytes accessed | tf_op | source)
XLA Modules:
  0.0 112.3 jit_solution(1119500769556721474)
XLA Ops:
  0.6 109.1 %expert_backward.1 = (bf16[64,2048]{1,0:T(8,128)(2,1)}, f32[256,768]{1,0:T(8,128)}, f32[256,768]{1,0:T(8,128)}) custom-call(s32[8,64]{1,0:T(8,128)} %bitcast.9, bf16[64,2048]{1,0:T(8,128)(2,1)} %x_hbm.1, bf16[512,768]{1,0:T(8,128)(2,1)} %bitcast.8, bf16[2048,768]{1,0:T(8,128)(2,1)} %bitcast.6, bf16[2048,768]{1,0:T(8,128)(2,1)} %bitcast.7), custom_call_target="tpu_custom_call" | custom-call | tf_op jit(solution)/shard_map/expert_backward/pallas_call | solution.py:533
  109.8 2.4 %hand_over.1 = (bf16[64,2048]{1,0:T(8,128)(2,1)}, f32[256,768]{1,0:T(8,128)}, f32[256,768]{1,0:T(8,128)}) custom-call(bf16[64,2048]{1,0:T(8,128)(2,1)} %get-tuple-element.9.a, f32[256,768]{1,0:T(8,128)} %get-tuple-element.10.b, f32[256,768]{1,0:T(8,128)} %get-tuple-element.11.c), custom_call_target="tpu_custom_call" | custom-call | tf_op jit(solution)/shard_map/hand_over/pallas_call | solution.py:586

commit v8 on v7

--- a/solution.py
+++ b/solution.py
@@ -223,8 +223,6 @@
         return c
 
     lax.fori_loop(0, n_ex // lot, pack, 0)
-    to_peers(lambda t: dh_copy(t, me, 0).start())
-    keep_own(dh_piece(dh_out.at[me], 0), dh_piece(dh_in.at[me], 0), dh_recv.at[0])
 
     both_ways = [(h, sign) for h in range(2) for sign in (1, -1)]
     for h, sign in both_ways:
@@ -244,6 +242,9 @@
         for sign in (1, -1):
             pass_on(h, 2, 0, 1, sign)
         share(h, 2, 0)
+
+    to_peers(lambda t: dh_copy(t, me, 0).start())
+    keep_own(dh_piece(dh_out.at[me], 0), dh_piece(dh_in.at[me], 0), dh_recv.at[0])
 
     landed(all_ref, r_recv)
     for s in range(n_ex):

time: 112 us -> 112 us (level)
  no operation moved by 1% of the time
where the time goes in v8:
time: 112 us
  Pallas kernels  111 us (99%)
    pallas_call x1, Pallas kernels, body(): pl.pallas_call(functools.partial(expert_kernel, (n_dp, n_ex, slots, tok,...  109 us
    pallas_call x1, Pallas kernels, body(): pl.pallas_call(hand_over, out_shape=tuple((jax.ShapeDtypeStruct(g.shape,...  2.41 us

profile of v8, /device:TPU:1, one launch (start us, length us, event | category | flops | bytes accessed | tf_op | source)
XLA Modules:
  0.0 111.7 jit_solution(6506377797760253670)
XLA Ops:
  0.6 108.5 %expert_backward.1 = (bf16[64,2048]{1,0:T(8,128)(2,1)}, f32[256,768]{1,0:T(8,128)}, f32[256,768]{1,0:T(8,128)}) custom-call(s32[8,64]{1,0:T(8,128)} %bitcast.9, bf16[64,2048]{1,0:T(8,128)(2,1)} %x_hbm.1, bf16[512,768]{1,0:T(8,128)(2,1)} %bitcast.8, bf16[2048,768]{1,0:T(8,128)(2,1)} %bitcast.6, bf16[2048,768]{1,0:T(8,128)(2,1)} %bitcast.7), custom_call_target="tpu_custom_call" | custom-call | tf_op jit(solution)/shard_map/expert_backward/pallas_call | solution.py:534
  109.1 2.4 %hand_over.1 = (bf16[64,2048]{1,0:T(8,128)(2,1)}, f32[256,768]{1,0:T(8,128)}, f32[256,768]{1,0:T(8,128)}) custom-call(bf16[64,2048]{1,0:T(8,128)(2,1)} %get-tuple-element.9.a, f32[256,768]{1,0:T(8,128)} %get-tuple-element.10.b, f32[256,768]{1,0:T(8,128)} %get-tuple-element.11.c), custom_call_target="tpu_custom_call" | custom-call | tf_op jit(solution)/shard_map/hand_over/pallas_call | solution.py:587
